TPU v7x, 1024 devices: a whole 4x4x32 slice. The times are simulated.
1024 devices in a mesh: dp: 16 (over y, x_hi, core), shard: 64 (over x_lo, z).
Axes of the slice: x: 4 (x_hi: 2, x_lo: 2; x = x_hi * 2 + x_lo), y: 4, z: 32, core: 2. Of those that a mesh axis runs over, the one named last changes fastest.
Arguments:
- feats: bfloat16 [524288, 3072], P(('dp', 'shard')), may hold values from -24 to 24
- w_qkv: bfloat16 [3072, 384], P('shard'), may hold values from -0.125 to 0.125
- grad_out: bfloat16 [524288, 128], P(('dp', 'shard')), may hold values from -6 to 6
- block_mask: int32 [1024, 4, 4], P(('dp', 'shard')), may hold values from 0 to 1, as said below
- counts: int32 [1024], P(('dp', 'shard')), may hold values from 128 to 512
Outputs:
- attended: bfloat16 [524288, 128], P(('dp', 'shard'))
- grad_w: float32 [3072, 384], P('shard')
Inputs may be any that keep to these rules, and one draw needn't show every extreme that they name: block_mask[c, b, 0] and block_mask[c, b, b] are 1 for every block b.
All inputs are finite; a program needn't handle non-finite values.
Results may differ from a plain program's by a relative error of at most 0.029.
Values may be sent and summed in bfloat16 or wider, within the bound.
No kernel may reach another device: no remote copies, remote signals or barrier semaphores. Data moves between devices by JAX's collectives and lax.ppermute only.
A program may use at most 32 MiB of HBM per device.

v0:
```python
import jax
import jax.numpy as jnp
from jax import lax
from jax.sharding import PartitionSpec as P


def attention_pass(qkv, cotangent, mask, count, length, block, head):
    query = qkv[:, :head]
    keys = qkv[:, head : 2 * head]
    values = qkv[:, 2 * head :]
    factor = 1.0 / jnp.sqrt(jnp.float32(head))
    scores = jnp.dot(query, keys.T, preferred_element_type=jnp.float32) * factor
    expanded = jnp.repeat(jnp.repeat(mask, block, axis=0), block, axis=1)
    position = jnp.arange(length, dtype=jnp.int32)
    live = (expanded > 0) & (position[None, :] < count)
    scores = jnp.where(live, scores, jnp.float32(-1e30))
    top = jnp.max(scores, axis=1, keepdims=True)
    weight = jnp.where(live, jnp.exp(scores - top), jnp.float32(0.0))
    probs = weight / jnp.sum(weight, axis=1, keepdims=True)
    probs_b = probs.astype(jnp.bfloat16)
    output = jnp.dot(probs_b, values, preferred_element_type=jnp.float32).astype(jnp.bfloat16)
    grad_values = jnp.dot(probs_b.T, cotangent, preferred_element_type=jnp.float32)
    dprobs = jnp.dot(cotangent, values.T, preferred_element_type=jnp.float32)
    delta = jnp.sum(
        cotangent.astype(jnp.float32) * output.astype(jnp.float32), axis=1, keepdims=True
    )
    dscore = (probs * (dprobs - delta) * factor).astype(jnp.bfloat16)
    grad_query = jnp.dot(dscore, keys, preferred_element_type=jnp.float32)
    grad_keys = jnp.dot(dscore.T, query, preferred_element_type=jnp.float32)
    d_qkv = jnp.concatenate([grad_query, grad_keys, grad_values], axis=1).astype(jnp.bfloat16)
    return (output, d_qkv)


def contract_rows(columns, d_qkv):
    return lax.dot_general(
        columns, d_qkv, (((0,), (0,)), ((), ())), preferred_element_type=jnp.float32
    )


def on_device(feats, w_qkv, grad_out, block_mask, counts):
    length = feats.shape[0]
    head = grad_out.shape[1]
    block = length // block_mask.shape[1]
    columns = feats
    qkv = jnp.dot(
        columns,
        lax.all_gather(w_qkv, "shard", axis=0, tiled=True),
        preferred_element_type=jnp.float32,
    ).astype(jnp.bfloat16)
    attended, d_qkv = attention_pass(qkv, grad_out, block_mask[0], counts[0], length, block, head)
    columns = feats
    owned = lax.psum_scatter(
        contract_rows(columns, d_qkv), "shard", scatter_dimension=0, tiled=True
    )
    grad_w = lax.psum(owned.astype(jnp.bfloat16), "dp").astype(jnp.float32)
    return (attended, grad_w)


def solution(mesh):
    return jax.shard_map(
        on_device,
        mesh=mesh,
        in_specs=(
            P(("dp", "shard"), None),
            P("shard", None),
            P(("dp", "shard"), None),
            P(("dp", "shard"), None, None),
            P(("dp", "shard")),
        ),
        out_specs=(P(("dp", "shard"), None), P("shard", None)),
        check_vma=False,
    )
```

profile of v0, /device:TPU:1, one launch (start us, length us, event | category | flops | bytes accessed | tf_op | source)
XLA Modules:
  0.0 620.4 jit_solution(7006671510071690204)
XLA Ops:
  7.2 0.0 copy-start
  7.2 0.0 all-gather.2.cloned.1.call-start
  7.2 0.7 all-gather.2.cloned.1.call-update
  7.9 0.0 reduce-scatter.4.cloned.1.call-start
  8.8 0.7 compare_bitcast_fusion
  9.5 0.1 copy.11
  9.6 0.1 broadcast_bitcast_fusion
  9.7 1.0 copy.12
  10.7 0.2 bitcast_and_fusion
  10.9 223.4 %all-gather.2.cloned.1.call-done = bf16[3072,384]{1,0:T(8,128)(2,1)} async-done(((bf16[48,384]{1,0:T(8,128)(2,1)}), bf16[3072,384]{1,0:T(8,128)(2,1)}) %all-gather.2.cloned.1.call-update) | async-done | bytes 2359312 | tf_op jit(solution)/shard_map/all_gather | solution.py:47
  234.3 0.0 copy-done
  234.3 3.4 convolution_convert_fusion
  237.7 0.0 copy-start.1
  237.7 0.3 fusion.21
  238.1 0.3 fusion.6
  238.4 0.3 fusion.5
  238.6 0.0 copy-done.1
  238.6 0.3 convolution_convert_fusion.1
  238.9 0.3 multiply_reduce_fusion
  239.2 0.3 fusion.4
  239.5 0.3 convolution_convert_fusion.2
  239.8 0.4 convolution_convert_fusion.3
  240.2 3.6 convolution_bitcast_fusion
  243.8 6.0 copy.15
  249.8 0.0 reduce-scatter.4.cloned.1.call-update
  249.9 0.8 copy.13
  250.6 254.7 %reduce-scatter.4.cloned.1.call-done = f32[48,384]{1,0:T(8,128)} async-done(((f32[3072,384]{1,0:T(8,128)}), f32[48,384]{1,0:T(8,128)}) %reduce-scatter.4.cloned.1.call-update) | async-done | bytes 73744
  505.3 1.0 copy.16
  506.4 106.5 %psum.7 = bf16[48,384]{0,1:T(8,128)(2,1)S(1)} all-reduce(bf16[48,384]{0,1:T(8,128)(2,1)S(1)} %copy.16), channel_id=1, replica_groups=mesh['dp'=16,'shard'=64] {'dp'}, use_global_device_ids=true, to_apply=%region_4.5 | all-reduce | flops 18432 | bytes 73728 | tf_op jit(solution)/shard_map/psum | solution.py:55
  612.9 0.7 copy.14
  (2 shorter events, 0.0 us)
Async XLA Ops:
  7.2 227.1 %copy-start = (bf16[512,3072]{1,0:T(8,128)(2,1)S(1)}, bf16[512,3072]{1,0:T(8,128)(2,1)}, u32[]{:S(2)}) copy-start(bf16[512,3072]{1,0:T(8,128)(2,1)} %param.5) | copy-start | bytes 9437188
  7.2 227.1 %all-gather.2.cloned.1.call-start = ((), (), s32[]{:S(2)}) async-start(), calls=%async_computation.1 | async-start | bytes 2396160 | tf_op jit(solution)/shard_map/all_gather | solution.py:47
  7.9 497.4 %reduce-scatter.4.cloned.1.call-start = ((), (), s32[]{:S(2)}) async-start(), calls=%async_computation.2 | async-start | bytes 4792320
  237.7 0.9 copy-start.1
Sparse Core Ops, SparseCore 0:
  10.7 223.5 all-gather.1
  250.0 255.3 reduce-scatter.3
where the time goes:
time: 624 us; the launch traced here: 620 us
  waiting for transfers between devices  479 us (77%)
  blocking collectives  107 us (17%)
  between operations  14.9 us (2%)
  local copies, waits for them, and re-layouts  9.74 us (2%)
  matrix products  8.91 us (1%)
    unnamed x3, waiting for transfers between devices  255 us
    all_gather x1, waiting for transfers between devices, on_device(): lax.all_gather(w_qkv, 'shard', axis=0, tiled=True)  223 us
    psum x1, blocking collectives, on_device(): grad_w = lax.psum(owned.astype(jnp.bfloat16), 'dp').astype(jnp.float32)  107 us
  transfers between devices with their start and end apart: 2, of which 2 were waited for; matrix products, arithmetic and copies ran while one was open for 0% of the time, Pallas kernels for 0%

commit v1 on v0

v1 whole, which is shorter than its diff:
```python
import jax
import jax.numpy as jnp
from jax import lax
from jax.sharding import Mesh
from jax.sharding import PartitionSpec as P

BF16 = jnp.bfloat16
F32 = jnp.float32
DP = ("y", "xh", "core")
SHARD = ("xl", "z")
CHIPS = ("xl", "y", "xh")
SWAP = [(0, 1), (1, 0)]


def attention_pass(qkv, cotangent, mask, count, length, block, head):
    query = qkv[:, :head]
    keys = qkv[:, head : 2 * head]
    values = qkv[:, 2 * head :]
    factor = 1.0 / jnp.sqrt(F32(head))
    scores = jnp.dot(query, keys.T, preferred_element_type=F32) * factor
    expanded = jnp.repeat(jnp.repeat(mask, block, axis=0), block, axis=1)
    position = jnp.arange(length, dtype=jnp.int32)
    live = (expanded > 0) & (position[None, :] < count)
    scores = jnp.where(live, scores, F32(-1e30))
    top = jnp.max(scores, axis=1, keepdims=True)
    weight = jnp.where(live, jnp.exp(scores - top), F32(0.0))
    probs = weight / jnp.sum(weight, axis=1, keepdims=True)
    probs_b = probs.astype(BF16)
    output = jnp.dot(probs_b, values, preferred_element_type=F32).astype(BF16)
    grad_values = jnp.dot(probs_b.T, cotangent, preferred_element_type=F32)
    dprobs = jnp.dot(cotangent, values.T, preferred_element_type=F32)
    delta = jnp.sum(cotangent.astype(F32) * output.astype(F32), axis=1, keepdims=True)
    dscore = (probs * (dprobs - delta) * factor).astype(BF16)
    grad_query = jnp.dot(dscore, keys, preferred_element_type=F32)
    grad_keys = jnp.dot(dscore.T, query, preferred_element_type=F32)
    d_qkv = jnp.concatenate([grad_query, grad_keys, grad_values], axis=1).astype(BF16)
    return (output, d_qkv)


def contract_rows(columns, d_qkv):
    return lax.dot_general(columns, d_qkv, (((0,), (0,)), ((), ())), preferred_element_type=F32)


def reordered(feats, core, n_xl, n_z, n_dp, unit):
    depth = feats.shape[1] // n_xl
    half = n_dp // 2
    line = n_z * unit
    at = lax.broadcasted_iota(jnp.int32, (depth, depth // 2), 1)
    pair, z, row = at // line, (at % line) // unit, at % unit
    source = z * (n_dp * unit) + (2 * pair + core) * unit + row
    pick = (lax.broadcasted_iota(jnp.int32, (depth, depth // 2), 0) == source).astype(BF16)
    blocks = [
        jnp.dot(feats[:, k * depth : (k + 1) * depth], pick, preferred_element_type=F32).astype(BF16)
        for k in range(n_xl)
    ]
    return jnp.concatenate(blocks, axis=1)


def on_device(feats, w_qkv, grad_out, block_mask, counts):
    length = feats.shape[0]
    head = grad_out.shape[1]
    block = length // block_mask.shape[1]
    n_xl, n_z, n_dp = lax.axis_size("xl"), lax.axis_size("z"), lax.axis_size(DP)
    chips = lax.axis_size(CHIPS)
    rows, width = w_qkv.shape
    unit = rows // n_dp
    core = lax.axis_index("core")

    piece = lax.dynamic_slice_in_dim(w_qkv, lax.axis_index(DP) * unit, unit, axis=0)
    line = lax.all_to_all(jnp.broadcast_to(piece, (n_z, unit, width)), "z", 0, 0, tiled=True)
    line = line.reshape(n_z * unit, width)
    own_w = lax.all_to_all(jnp.broadcast_to(line, (chips,) + line.shape), CHIPS, 0, 0, tiled=True)
    own_w = own_w.reshape(chips * n_z * unit, width)
    other_w = lax.ppermute(own_w, "core", SWAP)

    own_feats = reordered(feats, core, n_xl, n_z, n_dp, unit)
    other_feats = reordered(feats, 1 - core, n_xl, n_z, n_dp, unit)
    qkv = jnp.dot(own_feats, own_w, preferred_element_type=F32)
    qkv = (qkv + jnp.dot(other_feats, other_w, preferred_element_type=F32)).astype(BF16)
    attended, d_qkv = attention_pass(qkv, grad_out, block_mask[0], counts[0], length, block, head)

    passed = lax.ppermute(contract_rows(other_feats, d_qkv).astype(BF16), "core", SWAP)
    chip = (contract_rows(own_feats, d_qkv) + passed.astype(F32)).astype(BF16)
    plane = lax.all_to_all(chip.reshape(chips, n_z * unit, width), CHIPS, 0, 0, tiled=True)
    plane = jnp.sum(plane.astype(F32), axis=0).astype(BF16)
    owned = lax.all_to_all(plane.reshape(n_z, unit, width), "z", 0, 0, tiled=True)
    owned = jnp.sum(owned.astype(F32), axis=0).astype(BF16)
    grad_w = lax.all_to_all(jnp.broadcast_to(owned, (n_dp, unit, width)), DP, 0, 0, tiled=True)
    return (attended, grad_w.reshape(rows, width).astype(F32))


def solution(mesh):
    fine = Mesh(mesh.devices.reshape(4, 2, 2, 2, 32), DP + SHARD)
    split = DP + SHARD
    return jax.shard_map(
        on_device,
        mesh=fine,
        in_specs=(
            P(split, None),
            P(SHARD, None),
            P(split, None),
            P(split, None, None),
            P(split),
        ),
        out_specs=(P(split, None), P(SHARD, None)),
        check_vma=False,
    )
```

time: 624 us -> 170 us (0.27)
  waiting for transfers between devices: 479 us -> 40.7 us
  blocking collectives: 107 us -> 50.9 us
  starting transfers between devices: 0.08 us -> 52.6 us
  between operations: 14.9 us -> 1.55 us
  matrix products: 8.91 us -> 17 us
    unnamed x3 -> x0, waiting for transfers between devices: 255 us -> none
    all_gather x1 -> x0, waiting for transfers between devices: 223 us -> none  [on_device(): lax.all_gather(w_qkv, 'shard', axis=0, tiled=True)]
    psum x1 -> x0, blocking collectives: 107 us -> none  [on_device(): grad_w = lax.psum(owned.astype(jnp.bfloat16), 'dp').astype(jnp.float32)]
    all_to_all x0 -> x2, blocking collectives: none -> 50.9 us  [the longest x1 28.9 us: on_device(): lax.all_to_all(plane.reshape(n_z, unit, width), 'z', 0, 0, tiled=True)]
    all_to_all x0 -> x3, starting transfers between devices: none -> 44.2 us  [the longest x1 29.3 us: on_device(): lax.all_to_all(jnp.broadcast_to(piece, (n_z, unit, width)), 'z', 0, 0, ti...]
    all_to_all x0 -> x3, waiting for transfers between devices: none -> 37.9 us  [the longest x1 20.8 us: on_device(): lax.all_to_all(jnp.broadcast_to(piece, (n_z, unit, width)), 'z', 0, 0, ti...]
    dot_general x7 -> x12, matrix products: 5.32 us -> 15 us  [the longest x4 11.1 us: reordered(): jnp.dot(feats[:, k * depth:(k + 1) * depth], pick, preferred_element_type...]
    ppermute x0 -> x2, starting transfers between devices: none -> 8.46 us  [the longest x1 6.54 us: on_device(): other_w = lax.ppermute(own_w, 'core', SWAP)]
  transfers between devices with their start and end apart: 2 -> 5, of which waited for: 2 -> 4; matrix products, arithmetic and copies ran while one was open for 0% -> 8% of each run, Pallas kernels for 0% -> 0%
where the time goes in v1:
time: 170 us; the launch traced here: 169 us
  starting transfers between devices  52.6 us (31%)
  blocking collectives  50.9 us (30%)
  waiting for transfers between devices  40.7 us (24%)
  matrix products  17 us (10%)
  local copies, waits for them, and re-layouts  5.14 us (3%)
    all_to_all x1, starting transfers between devices, on_device(): lax.all_to_all(jnp.broadcast_to(piece, (n_z, unit, width)), 'z', 0, 0, ti...  29.3 us
    all_to_all x1, blocking collectives, on_device(): lax.all_to_all(plane.reshape(n_z, unit, width), 'z', 0, 0, tiled=True)  28.9 us
    all_to_all x1, blocking collectives, on_device(): lax.all_to_all(chip.reshape(chips, n_z * unit, width), CHIPS, 0, 0, tiled...  22 us
    all_to_all x1, waiting for transfers between devices, on_device(): lax.all_to_all(jnp.broadcast_to(piece, (n_z, unit, width)), 'z', 0, 0, ti...  20.8 us
    dot_general x4, matrix products, reordered(): jnp.dot(feats[:, k * depth:(k + 1) * depth], pick, preferred_element_type...  11.1 us
    all_to_all x1, waiting for transfers between devices, on_device(): lax.all_to_all(jnp.broadcast_to(line, (chips,) + line.shape), CHIPS, 0, 0...  10.4 us
    all_to_all x1, starting transfers between devices, on_device(): lax.all_to_all(jnp.broadcast_to(owned, (n_dp, unit, width)), DP, 0, 0, ti...  8.15 us
    all_to_all x1, starting transfers between devices, on_device(): lax.all_to_all(jnp.broadcast_to(line, (chips,) + line.shape), CHIPS, 0, 0...  6.75 us
  transfers between devices with their start and end apart: 5, of which 4 were waited for; matrix products, arithmetic and copies ran while one was open for 8% of the time, Pallas kernels for 0%

profile of v1, /device:TPU:1, one launch (start us, length us, event | category | flops | bytes accessed | tf_op | source)
XLA Modules:
  0.0 169.0 jit_solution(8869788535853462278)
XLA Ops:
  0.6 0.0 copy-start
  0.7 0.7 copy-done
  1.4 0.7 broadcast_in_dim.28
  2.1 29.3 %all-to-all-start = ((bf16[32,3,384]{2,1,0:T(4,128)(2,1)}), bf16[32,3,384]{2,1,0:T(4,128)(2,1)S(1)}, u32[]{:S(2)}, u32[]{:S(2)}) async-start(bf16[32,3,384]{2,1,0:T(4,128)(2,1)} %broadcast_in_dim.28), calls=%async_computation | async-start | bytes 196608 | tf_op jit(solution)/shard_map/all_to_all | solution.py:70
  31.4 0.0 copy-start.3
  31.5 3.0 %fusion.19 = bf16[512,768]{0,1:T(8,128)(2,1)S(1)} fusion(bf16[512,3072]{1,0:T(8,128)(2,1)} %param.5, s32[768]{0:T(1024)S(1)} %get-tuple-element.11, s32[768]{0:T(1024)S(1)} %get-tuple-element.12, s32[]{:T(128)S(6)} %axis_index.39, s32[768]{0:T(1024)S(1)} %get-tuple-element.10, s32[768]{0:T(1024)S(1)} %get-tuple-element.15, pred[768]{0:T(1024)(128)(4,1)S(1)} %fusion.55, ...), kind=kOutput, calls=%fused_computation.34 | convolution fusion | flops 1230766080 | bytes 2380036 | tf_op jit(solution)/shard_map/dot_general | solution.py:53
  34.5 0.0 copy-done.3
  34.5 0.0 copy-start.1
  34.5 0.0 copy-start.2
  34.5 1.4 fusion.16
  36.0 0.1 copy.11
  36.8 0.1 copy.10
  36.9 0.1 broadcast_bitcast_fusion
  37.0 0.2 bitcast_and_fusion
  37.2 20.8 %all-to-all-done = bf16[32,3,384]{2,1,0:T(4,128)(2,1)S(1)} async-done(((bf16[32,3,384]{2,1,0:T(4,128)(2,1)}), bf16[32,3,384]{2,1,0:T(4,128)(2,1)S(1)}, u32[]{:S(2)}, u32[]{:S(2)}) %all-to-all-start) | async-done | bytes 73760 | tf_op jit(solution)/shard_map/all_to_all | solution.py:70
  58.0 0.1 reshape.35
  58.1 1.1 broadcast_in_dim.29
  59.2 6.8 %all-to-all-start.1 = ((bf16[16,96,384]{2,1,0:T(8,128)(2,1)}), bf16[16,96,384]{2,1,0:T(8,128)(2,1)S(1)}, u32[]{:S(2)}, u32[]{:S(2)}) async-start(bf16[16,96,384]{2,1,0:T(8,128)(2,1)} %broadcast_in_dim.29), calls=%async_computation.1 | async-start | bytes 2359296 | tf_op jit(solution)/shard_map/all_to_all | solution.py:72
  66.0 3.8 %fusion.25 = bf16[512,768]{0,1:T(8,128)(2,1)} fusion(bf16[512,3072]{1,0:T(8,128)(2,1)} %param.5, s32[]{:T(128)S(6)} %sub.43, s32[768]{0:T(1024)S(1)} %get-tuple-element.11, s32[768]{0:T(1024)S(1)} %get-tuple-element.12, s32[768]{0:T(1024)S(1)} %get-tuple-element.10, s32[768]{0:T(1024)S(1)} %get-tuple-element.15, pred[768]{0:T(1024)(128)(4,1)S(1)} %fusion.55, ...), kind=kOutput, calls=%fused_computation.36 | convolution fusion | flops 1230766080 | bytes 2380036 | tf_op jit(solution)/shard_map/dot_general | solution.py:53
  69.8 10.4 %all-to-all-done.1 = bf16[16,96,384]{2,1,0:T(8,128)(2,1)S(1)} async-done(((bf16[16,96,384]{2,1,0:T(8,128)(2,1)}), bf16[16,96,384]{2,1,0:T(8,128)(2,1)S(1)}, u32[]{:S(2)}, u32[]{:S(2)}) %all-to-all-start.1) | async-done | bytes 1179680 | tf_op jit(solution)/shard_map/all_to_all | solution.py:72
  80.2 6.5 %collective-permute-start = (bf16[1536,384]{1,0:T(8,128)(2,1)S(1)}, bf16[1536,384]{1,0:T(8,128)(2,1)S(1)}, u32[]{:S(2)}, u32[]{:S(2)}) collective-permute-start(bf16[1536,384]{1,0:T(8,128)(2,1)S(1)} %bitcast.41), channel_id=1, source_target_pairs={{0,64},{64,0},{1,65},{65,1},{2,66},{66,2},{3,67},{67,3},{4,68},{68... | collective-permute-start | bytes 3538952 | tf_op jit(solution)/shard_map/ppermute | solution.py:74
  86.7 2.9 %fusion.22 = bf16[512,768]{0,1:T(8,128)(2,1)S(1)} fusion(bf16[512,3072]{1,0:T(8,128)(2,1)} %param.5, s32[]{:T(128)S(6)} %sub.43, s32[768]{0:T(1024)S(1)} %get-tuple-element.11, s32[768]{0:T(1024)S(1)} %get-tuple-element.12, s32[768]{0:T(1024)S(1)} %get-tuple-element.10, s32[768]{0:T(1024)S(1)} %get-tuple-element.15, pred[768]{0:T(1024)(128)(4,1)S(1)} %fusion.55, ...), kind=kOutput, calls=%fused_computation.35 | convolution fusion | flops 1230766080 | bytes 2380036 | tf_op jit(solution)/shard_map/dot_general | solution.py:53
  89.6 0.0 copy-start.4
  89.6 1.0 fusion.31
  90.6 0.0 collective-permute-done
  90.6 0.1 copy-done.4
  90.7 1.0 fusion.29
  91.8 0.3 fusion.84
  92.1 0.3 fusion.37
  92.4 0.3 fusion.36
  92.6 0.3 convolution_convert_fusion.5
  93.0 0.3 multiply_reduce_fusion
  93.3 0.3 fusion.28
  93.6 0.3 convolution_convert_fusion.6
  93.9 0.3 convolution_convert_fusion.7
  94.2 1.0 convolution_convert_fusion
  95.2 1.9 %collective-permute-start.1 = (bf16[1536,384]{1,0:T(8,128)(2,1)S(1)}, bf16[1536,384]{1,0:T(8,128)(2,1)S(1)}, u32[]{:S(2)}, u32[]{:S(2)}) collective-permute-start(bf16[1536,384]{1,0:T(8,128)(2,1)S(1)} %convolution_convert_fusion), channel_id=1, source_target_pairs={{0,64},{64,0},{1,65},{65,1},{2,66},{66,2},{3,67},{67,3},{4,68},{68... | collective-permute-start | bytes 3538952 | tf_op jit(solution)/shard_map/ppermute | solution.py:82
  97.1 2.8 %collective-permute-done.1 = bf16[1536,384]{1,0:T(8,128)(2,1)S(1)} collective-permute-done((bf16[1536,384]{1,0:T(8,128)(2,1)S(1)}, bf16[1536,384]{1,0:T(8,128)(2,1)S(1)}, u32[]{:S(2)}, u32[]{:S(2)}) %collective-permute-start.1) | collective-permute-done | bytes 1179680 | tf_op jit(solution)/shard_map/ppermute | solution.py:82
  99.9 1.0 add_convert_fusion
  100.9 22.0 %all_to_all.25 = bf16[16,96,384]{2,1,0:T(8,128)(2,1)S(1)} all-to-all(bf16[16,96,384]{2,1,0:T(8,128)(2,1)S(1)} %bitcast.43), channel_id=1, replica_groups=mesh['y'=4,'xh'=2,'core'=2,'xl'=2,'z'=32] {'xl','y','xh'}, dimensions={0} | all-to-all | bytes 2359296 | tf_op jit(solution)/shard_map/all_to_all | solution.py:84
  122.9 0.2 reduce_sum.44
  123.2 28.9 %all_to_all.26 = bf16[32,3,384]{2,1,0:T(4,128)(2,1)S(1)} all-to-all(bf16[32,3,384]{2,1,0:T(4,128)(2,1)S(1)} %reshape.38), channel_id=1, replica_groups=mesh['y'=4,'xh'=2,'core'=2,'xl'=2,'z'=32] {'z'}, dimensions={0} | all-to-all | bytes 147456 | tf_op jit(solution)/shard_map/all_to_all | solution.py:86
  152.1 0.1 reduce_sum.45
  152.1 0.6 broadcast_in_dim.32
  152.8 8.2 %all-to-all-start.4 = ((bf16[16,3,384]{2,1,0:T(4,128)(2,1)}), bf16[16,3,384]{2,1,0:T(4,128)(2,1)S(1)}, u32[]{:S(2)}, u32[]{:S(2)}) async-start(bf16[16,3,384]{2,1,0:T(4,128)(2,1)} %broadcast_in_dim.32), calls=%async_computation.4 | async-start | bytes 98304 | tf_op jit(solution)/shard_map/all_to_all | solution.py:88
  160.9 0.8 copy.12
  161.7 6.6 %all-to-all-done.4 = bf16[16,3,384]{2,1,0:T(4,128)(2,1)S(1)} async-done(((bf16[16,3,384]{2,1,0:T(4,128)(2,1)}), bf16[16,3,384]{2,1,0:T(4,128)(2,1)S(1)}, u32[]{:S(2)}, u32[]{:S(2)}) %all-to-all-start.4) | async-done | bytes 36896 | tf_op jit(solution)/shard_map/all_to_all | solution.py:88
  168.3 0.7 reshape.39
  (12 shorter events, 0.1 us)
Async XLA Ops:
  0.6 0.8 copy-start
  2.1 55.9 %all-to-all-start = ((bf16[32,3,384]{2,1,0:T(4,128)(2,1)}), bf16[32,3,384]{2,1,0:T(4,128)(2,1)S(1)}, u32[]{:S(2)}, u32[]{:S(2)}) async-start(bf16[32,3,384]{2,1,0:T(4,128)(2,1)} %broadcast_in_dim.28), calls=%async_computation | async-start | bytes 196608 | tf_op jit(solution)/shard_map/all_to_all | solution.py:70
  31.4 3.0 %copy-start.3 = (bf16[512,3072]{1,0:T(8,128)(2,1)S(1)}, bf16[512,3072]{1,0:T(8,128)(2,1)}, u32[]{:S(2)}) copy-start(bf16[512,3072]{1,0:T(8,128)(2,1)} %param.5) | copy-start | bytes 9437188
  34.5 1.5 copy-start.1
  34.5 2.3 %copy-start.2 = (s32[1,4,4]{2,1,0:T(4,128)S(1)}, s32[1,4,4]{2,1,0:T(4,128)}, u32[]{:S(2)}) copy-start(s32[1,4,4]{2,1,0:T(4,128)} %param.8) | copy-start | bytes 196
  59.2 21.0 %all-to-all-start.1 = ((bf16[16,96,384]{2,1,0:T(8,128)(2,1)}), bf16[16,96,384]{2,1,0:T(8,128)(2,1)S(1)}, u32[]{:S(2)}, u32[]{:S(2)}) async-start(bf16[16,96,384]{2,1,0:T(8,128)(2,1)} %broadcast_in_dim.29), calls=%async_computation.1 | async-start | bytes 2359296 | tf_op jit(solution)/shard_map/all_to_all | solution.py:72
  80.2 10.5 %collective-permute-start = (bf16[1536,384]{1,0:T(8,128)(2,1)S(1)}, bf16[1536,384]{1,0:T(8,128)(2,1)S(1)}, u32[]{:S(2)}, u32[]{:S(2)}) collective-permute-start(bf16[1536,384]{1,0:T(8,128)(2,1)S(1)} %bitcast.41), channel_id=1, source_target_pairs={{0,64},{64,0},{1,65},{65,1},{2,66},{66,2},{3,67},{67,3},{4,68},{68... | collective-permute-start | bytes 3538952 | tf_op jit(solution)/shard_map/ppermute | solution.py:74
  89.6 1.1 copy-start.4
  95.2 4.7 %collective-permute-start.1 = (bf16[1536,384]{1,0:T(8,128)(2,1)S(1)}, bf16[1536,384]{1,0:T(8,128)(2,1)S(1)}, u32[]{:S(2)}, u32[]{:S(2)}) collective-permute-start(bf16[1536,384]{1,0:T(8,128)(2,1)S(1)} %convolution_convert_fusion), channel_id=1, source_target_pairs={{0,64},{64,0},{1,65},{65,1},{2,66},{66,2},{3,67},{67,3},{4,68},{68... | collective-permute-start | bytes 3538952 | tf_op jit(solution)/shard_map/ppermute | solution.py:82
  152.8 15.5 %all-to-all-start.4 = ((bf16[16,3,384]{2,1,0:T(4,128)(2,1)}), bf16[16,3,384]{2,1,0:T(4,128)(2,1)S(1)}, u32[]{:S(2)}, u32[]{:S(2)}) async-start(bf16[16,3,384]{2,1,0:T(4,128)(2,1)} %broadcast_in_dim.32), calls=%async_computation.4 | async-start | bytes 98304 | tf_op jit(solution)/shard_map/all_to_all | solution.py:88

commit v2 on v1

--- a/solution.py
+++ b/solution.py
@@ -7,8 +7,9 @@
 BF16 = jnp.bfloat16
 F32 = jnp.float32
 DP = ("y", "xh", "core")
-SHARD = ("xl", "z")
+SHARD = ("xl", "zh", "zl")
 CHIPS = ("xl", "y", "xh")
+REPLICAS = ("y", "xh")
 SWAP = [(0, 1), (1, 0)]
 
 
@@ -41,12 +42,12 @@
     return lax.dot_general(columns, d_qkv, (((0,), (0,)), ((), ())), preferred_element_type=F32)
 
 
-def reordered(feats, core, n_xl, n_z, n_dp, unit):
+def reordered(feats, core, n_xl, n_zh, n_zl, n_dp, unit):
     depth = feats.shape[1] // n_xl
-    half = n_dp // 2
-    line = n_z * unit
+    line = n_zl * n_zh * unit
     at = lax.broadcasted_iota(jnp.int32, (depth, depth // 2), 1)
-    pair, z, row = at // line, (at % line) // unit, at % unit
+    pair, row = at // line, at % unit
+    z = (at // unit) % n_zh * n_zl + (at % line) // (n_zh * unit)
     source = z * (n_dp * unit) + (2 * pair + core) * unit + row
     pick = (lax.broadcasted_iota(jnp.int32, (depth, depth // 2), 0) == source).astype(BF16)
     blocks = [
@@ -60,37 +61,44 @@
     length = feats.shape[0]
     head = grad_out.shape[1]
     block = length // block_mask.shape[1]
-    n_xl, n_z, n_dp = lax.axis_size("xl"), lax.axis_size("z"), lax.axis_size(DP)
-    chips = lax.axis_size(CHIPS)
+    n_xl, n_zh, n_zl, n_dp = (lax.axis_size(axes) for axes in ("xl", "zh", "zl", DP))
+    chips, replicas, cores = (lax.axis_size(axes) for axes in (CHIPS, REPLICAS, "core"))
     rows, width = w_qkv.shape
     unit = rows // n_dp
+    line_rows = n_zl * n_zh * unit
     core = lax.axis_index("core")
 
     piece = lax.dynamic_slice_in_dim(w_qkv, lax.axis_index(DP) * unit, unit, axis=0)
-    line = lax.all_to_all(jnp.broadcast_to(piece, (n_z, unit, width)), "z", 0, 0, tiled=True)
-    line = line.reshape(n_z * unit, width)
+    far = lax.all_to_all(jnp.broadcast_to(piece, (n_zh, unit, width)), "zh", 0, 0, tiled=True)
+    far = far.reshape(n_zh * unit, width)
+    line = lax.all_to_all(jnp.broadcast_to(far, (n_zl,) + far.shape), "zl", 0, 0, tiled=True)
+    line = line.reshape(line_rows, width)
+    own_feats = reordered(feats, core, n_xl, n_zh, n_zl, n_dp, unit)
+    other_feats = reordered(feats, 1 - core, n_xl, n_zh, n_zl, n_dp, unit)
+    line, own_feats, other_feats = lax.optimization_barrier((line, own_feats, other_feats))
     own_w = lax.all_to_all(jnp.broadcast_to(line, (chips,) + line.shape), CHIPS, 0, 0, tiled=True)
-    own_w = own_w.reshape(chips * n_z * unit, width)
+    own_w = own_w.reshape(chips * line_rows, width)
     other_w = lax.ppermute(own_w, "core", SWAP)
 
-    own_feats = reordered(feats, core, n_xl, n_z, n_dp, unit)
-    other_feats = reordered(feats, 1 - core, n_xl, n_z, n_dp, unit)
     qkv = jnp.dot(own_feats, own_w, preferred_element_type=F32)
     qkv = (qkv + jnp.dot(other_feats, other_w, preferred_element_type=F32)).astype(BF16)
     attended, d_qkv = attention_pass(qkv, grad_out, block_mask[0], counts[0], length, block, head)
 
     passed = lax.ppermute(contract_rows(other_feats, d_qkv).astype(BF16), "core", SWAP)
     chip = (contract_rows(own_feats, d_qkv) + passed.astype(F32)).astype(BF16)
-    plane = lax.all_to_all(chip.reshape(chips, n_z * unit, width), CHIPS, 0, 0, tiled=True)
+    plane = lax.all_to_all(chip.reshape(chips, line_rows, width), CHIPS, 0, 0, tiled=True)
     plane = jnp.sum(plane.astype(F32), axis=0).astype(BF16)
-    owned = lax.all_to_all(plane.reshape(n_z, unit, width), "z", 0, 0, tiled=True)
-    owned = jnp.sum(owned.astype(F32), axis=0).astype(BF16)
-    grad_w = lax.all_to_all(jnp.broadcast_to(owned, (n_dp, unit, width)), DP, 0, 0, tiled=True)
+    near = lax.all_to_all(plane.reshape(n_zl, n_zh * unit, width), "zl", 0, 0, tiled=True)
+    near = jnp.sum(near.astype(F32), axis=0).astype(BF16).reshape(n_zh, 1, unit, width)
+    near = jnp.broadcast_to(near, (n_zh, cores, unit, width)).reshape(n_zh * cores, unit, width)
+    owned = lax.all_to_all(near, ("zh", "core"), 0, 0, tiled=True)
+    owned = jnp.sum(owned.reshape(n_zh, cores * unit, width).astype(F32), axis=0).astype(BF16)
+    grad_w = lax.all_to_all(jnp.broadcast_to(owned, (replicas,) + owned.shape), REPLICAS, 0, 0, tiled=True)
     return (attended, grad_w.reshape(rows, width).astype(F32))
 
 
 def solution(mesh):
-    fine = Mesh(mesh.devices.reshape(4, 2, 2, 2, 32), DP + SHARD)
+    fine = Mesh(mesh.devices.reshape(4, 2, 2, 2, 4, 8), DP + SHARD)
     split = DP + SHARD
     return jax.shard_map(
         on_device,

time: 170 us -> 193 us (1.14)
  blocking collectives: 50.9 us -> 90.5 us
  waiting for transfers between devices: 40.7 us -> 28.1 us
  starting transfers between devices: 52.6 us -> 45.5 us
    all_to_all x2 -> x4, blocking collectives: 50.9 us -> 90.5 us  [the longest x1 35.5 us: on_device(): owned = lax.all_to_all(near, ('zh', 'core'), 0, 0, tiled=True)]
    all_to_all x3, waiting for transfers between devices: 37.9 us -> 25.2 us  [the longest x1 11.8 us: on_device(): lax.all_to_all(jnp.broadcast_to(piece, (n_zh, unit, width)), 'zh', 0, 0,...]
    all_to_all x3, starting transfers between devices: 44.2 us -> 36.9 us  [the longest x1 28.9 us: on_device(): lax.all_to_all(jnp.broadcast_to(piece, (n_zh, unit, width)), 'zh', 0, 0,...]
    dot_general x4, matrix products: 11.1 us -> 9.18 us  [reordered(): jnp.dot(feats[:, k * depth:(k + 1) * depth], pick, preferred_element_type...]
where the time goes in v2:
time: 193 us; the launch traced here: 192 us
  blocking collectives  90.5 us (47%)
  starting transfers between devices  45.5 us (24%)
  waiting for transfers between devices  28.1 us (15%)
  matrix products  17.6 us (9%)
  local copies, waits for them, and re-layouts  6.28 us (3%)
  other arithmetic  2.37 us (1%)
    all_to_all x1, blocking collectives, on_device(): owned = lax.all_to_all(near, ('zh', 'core'), 0, 0, tiled=True)  35.5 us
    all_to_all x1, starting transfers between devices, on_device(): lax.all_to_all(jnp.broadcast_to(piece, (n_zh, unit, width)), 'zh', 0, 0,...  28.9 us
    all_to_all x1, blocking collectives, on_device(): lax.all_to_all(jnp.broadcast_to(line, (chips,) + line.shape), CHIPS, 0, 0...  21.5 us
    all_to_all x1, blocking collectives, on_device(): lax.all_to_all(chip.reshape(chips, line_rows, width), CHIPS, 0, 0, tiled=...  20.7 us
    all_to_all x1, blocking collectives, on_device(): lax.all_to_all(plane.reshape(n_zl, n_zh * unit, width), 'zl', 0, 0, tiled...  12.8 us
    all_to_all x1, waiting for transfers between devices, on_device(): lax.all_to_all(jnp.broadcast_to(piece, (n_zh, unit, width)), 'zh', 0, 0,...  11.8 us
    dot_general x4, matrix products, reordered(): jnp.dot(feats[:, k * depth:(k + 1) * depth], pick, preferred_element_type...  9.18 us
    all_to_all x1, waiting for transfers between devices, on_device(): lax.all_to_all(jnp.broadcast_to(far, (n_zl,) + far.shape), 'zl', 0, 0, ti...  7.6 us
  transfers between devices with their start and end apart: 5, of which 4 were waited for; matrix products, arithmetic and copies ran while one was open for 8% of the time, Pallas kernels for 0%

profile of v2, /device:TPU:1, one launch (start us, length us, event | category | flops | bytes accessed | tf_op | source)
XLA Modules:
  0.0 191.9 jit_solution(10231933555074404951)
XLA Ops:
  0.6 0.0 copy-start
  0.7 0.7 copy-done
  1.4 0.6 broadcast_in_dim.38
  2.0 28.9 %all-to-all-start = ((bf16[4,3,384]{2,1,0:T(4,128)(2,1)}), bf16[4,3,384]{2,1,0:T(4,128)(2,1)S(1)}, u32[]{:S(2)}, u32[]{:S(2)}) async-start(bf16[4,3,384]{2,1,0:T(4,128)(2,1)} %broadcast_in_dim.38), calls=%async_computation | async-start | bytes 24576 | tf_op jit(solution)/shard_map/all_to_all | solution.py:72
  31.0 0.0 copy-start.5
  31.0 3.0 %fusion.25 = bf16[512,768]{0,1:T(8,128)(2,1)S(1)} fusion(bf16[512,3072]{1,0:T(8,128)(2,1)} %param.5, s32[]{:T(128)S(6)} %sub.53, s32[768]{0:T(1024)S(1)} %get-tuple-element.18, s32[768]{0:T(1024)S(1)} %get-tuple-element.19, s32[768]{0:T(1024)S(1)} %get-tuple-element.21, s32[768]{0:T(1024)S(1)} %get-tuple-element.26, ...), kind=kOutput, calls=%fused_computation.43 | convolution fusion | flops 1247281152 | bytes 2386948 | tf_op jit(solution)/shard_map/dot_general | solution.py:54
  34.0 1.5 fusion.28
  35.5 2.3 %fusion.19 = bf16[512,768]{0,1:T(8,128)(2,1)} fusion(bf16[512,3072]{1,0:T(8,128)(2,1)S(1)} %copy-done.5, s32[768]{0:T(1024)S(1)} %get-tuple-element.18, s32[768]{0:T(1024)S(1)} %get-tuple-element.19, s32[]{:T(128)S(6)} %axis_index.39, s32[768]{0:T(1024)S(1)} %get-tuple-element.21, s32[768]{0:T(1024)S(1)} %get-tuple-element.26, ...), kind=kOutput, calls=%fused_computation.41 | convolution fusion | flops 1247281152 | bytes 2396164 | tf_op jit(solution)/shard_map/dot_general | solution.py:54
  37.8 2.4 %fusion.22 = bf16[512,768]{0,1:T(8,128)(2,1)} fusion(bf16[512,3072]{1,0:T(8,128)(2,1)S(1)} %copy-done.5, s32[768]{0:T(1024)S(1)} %get-tuple-element.18, s32[768]{0:T(1024)S(1)} %get-tuple-element.19, s32[]{:T(128)S(6)} %axis_index.39, s32[768]{0:T(1024)S(1)} %get-tuple-element.21, s32[768]{0:T(1024)S(1)} %get-tuple-element.26, ...), kind=kOutput, calls=%fused_computation.42 | convolution fusion | flops 1247281152 | bytes 2396164 | tf_op jit(solution)/shard_map/dot_general | solution.py:54
  40.2 11.8 %all-to-all-done = bf16[4,3,384]{2,1,0:T(4,128)(2,1)S(1)} async-done(((bf16[4,3,384]{2,1,0:T(4,128)(2,1)}), bf16[4,3,384]{2,1,0:T(4,128)(2,1)S(1)}, u32[]{:S(2)}, u32[]{:S(2)}) %all-to-all-start) | async-done | bytes 9248 | tf_op jit(solution)/shard_map/all_to_all | solution.py:72
  52.0 0.7 broadcast_in_dim.39
  52.7 4.7 %all-to-all-start.1 = ((bf16[8,12,384]{2,1,0:T(8,128)(2,1)}), bf16[8,12,384]{2,1,0:T(8,128)(2,1)S(1)}, u32[]{:S(2)}, u32[]{:S(2)}) async-start(bf16[8,12,384]{2,1,0:T(8,128)(2,1)} %broadcast_in_dim.39), calls=%async_computation.1 | async-start | bytes 196608 | tf_op jit(solution)/shard_map/all_to_all | solution.py:74
  57.4 0.1 pad_maximum_fusion.1
  57.5 1.0 copy-done.2
  58.5 1.3 pad_maximum_fusion
  59.8 7.6 %all-to-all-done.1 = bf16[8,12,384]{2,1,0:T(8,128)(2,1)S(1)} async-done(((bf16[8,12,384]{2,1,0:T(8,128)(2,1)}), bf16[8,12,384]{2,1,0:T(8,128)(2,1)S(1)}, u32[]{:S(2)}, u32[]{:S(2)}) %all-to-all-start.1) | async-done | bytes 73760 | tf_op jit(solution)/shard_map/all_to_all | solution.py:74
  67.4 0.1 broadcast_in_dim.40
  67.5 21.5 %all_to_all.35 = bf16[16,96,384]{2,1,0:T(8,128)(2,1)} all-to-all(bf16[16,96,384]{2,1,0:T(8,128)(2,1)S(1)} %broadcast_in_dim.40), channel_id=1, replica_groups=mesh['y'=4,'xh'=2,'core'=2,'xl'=2,'zh'=4,'zl'=8] {'xl','y','xh'}, dimensions={0} | all-to-all | bytes 2359296 | tf_op jit(solution)/shard_map/all_to_all | solution.py:79
  89.0 6.7 %collective-permute-start = (bf16[1536,384]{1,0:T(8,128)(2,1)}, bf16[1536,384]{1,0:T(8,128)(2,1)}, u32[]{:S(2)}, u32[]{:S(2)}) collective-permute-start(bf16[1536,384]{1,0:T(8,128)(2,1)} %bitcast.7), channel_id=1, source_target_pairs={{0,64},{64,0},{1,65},{65,1},{2,66},{66,2},{3,67},{67,3},{4,68},{68... | collective-permute-start | bytes 3538952 | tf_op jit(solution)/shard_map/ppermute | solution.py:81
  95.7 0.1 copy.10
  95.8 0.1 broadcast_bitcast_fusion
  96.6 0.8 copy.11
  97.4 0.2 bitcast_and_fusion
  97.6 2.3 %fusion.62 = f32[512,384]{1,0:T(8,128)S(1)} fusion(bf16[512,1536]{0,1:T(8,128)(2,1)S(1)} %pad_maximum_fusion, bf16[1536,384]{1,0:T(8,128)(2,1)} %bitcast.7), kind=kOutput, calls=%fused_computation.93 | convolution fusion | flops 603979776 | bytes 3538944 | tf_op jit(solution)/shard_map/dot_general | solution.py:83
  99.8 0.0 collective-permute-done
  99.9 2.3 %fusion.32 = bf16[512,384]{1,0:T(8,128)(2,1)S(1)} fusion(f32[512,384]{1,0:T(8,128)S(1)} %fusion.62, bf16[512,1536]{0,1:T(8,128)(2,1)S(1)} %pad_maximum_fusion.1, bf16[1536,384]{1,0:T(8,128)(2,1)} %collective-permute-done), kind=kOutput, calls=%fused_computation.47 | convolution fusion | flops 604372992 | bytes 3932160 | tf_op jit(solution)/shard_map/dot_general | solution.py:84
  102.2 0.0 copy-start.3
  102.2 0.3 fusion.61
  102.5 0.3 fusion.34
  102.8 0.3 fusion.33
  103.1 0.3 multiply_reduce_fusion
  103.4 0.3 fusion.31
  103.7 0.3 convolution_convert_fusion.7
  104.0 0.3 convolution_convert_fusion.6
  104.3 0.3 convolution_convert_fusion.5
  104.6 1.0 convolution_convert_fusion
  105.6 1.9 %collective-permute-start.1 = (bf16[1536,384]{1,0:T(8,128)(2,1)S(1)}, bf16[1536,384]{1,0:T(8,128)(2,1)S(1)}, u32[]{:S(2)}, u32[]{:S(2)}) collective-permute-start(bf16[1536,384]{1,0:T(8,128)(2,1)S(1)} %convolution_convert_fusion), channel_id=1, source_target_pairs={{0,64},{64,0},{1,65},{65,1},{2,66},{66,2},{3,67},{67,3},{4,68},{68... | collective-permute-start | bytes 3538952 | tf_op jit(solution)/shard_map/ppermute | solution.py:87
  107.5 2.8 %collective-permute-done.1 = bf16[1536,384]{1,0:T(8,128)(2,1)S(1)} collective-permute-done((bf16[1536,384]{1,0:T(8,128)(2,1)S(1)}, bf16[1536,384]{1,0:T(8,128)(2,1)S(1)}, u32[]{:S(2)}, u32[]{:S(2)}) %collective-permute-start.1) | collective-permute-done | bytes 1179680 | tf_op jit(solution)/shard_map/ppermute | solution.py:87
  110.3 1.0 add_convert_fusion
  111.4 20.7 %all_to_all.36 = bf16[16,96,384]{2,1,0:T(8,128)(2,1)S(1)} all-to-all(bf16[16,96,384]{2,1,0:T(8,128)(2,1)S(1)} %bitcast.46), channel_id=1, replica_groups=mesh['y'=4,'xh'=2,'core'=2,'xl'=2,'zh'=4,'zl'=8] {'xl','y','xh'}, dimensions={0} | all-to-all | bytes 2359296 | tf_op jit(solution)/shard_map/all_to_all | solution.py:89
  132.1 0.2 reduce_sum.56
  132.3 12.8 %all_to_all.37 = bf16[8,12,384]{2,1,0:T(8,128)(2,1)S(1)} all-to-all(bf16[8,12,384]{2,1,0:T(8,128)(2,1)S(1)} %reshape.50), channel_id=1, replica_groups=mesh['y'=4,'xh'=2,'core'=2,'xl'=2,'zh'=4,'zl'=8] {'zl'}, dimensions={0} | all-to-all | bytes 147456 | tf_op jit(solution)/shard_map/all_to_all | solution.py:91
  145.2 35.5 %all_to_all.38 = bf16[8,3,384]{2,1,0:T(4,128)(2,1)S(1)} all-to-all(bf16[8,3,384]{2,1,0:T(4,128)(2,1)S(1)} %bitcast.47), channel_id=1, replica_groups=mesh['y'=4,'xh'=2,'core'=2,'xl'=2,'zh'=4,'zl'=8] {'zh','core'}, dimensions={0} | all-to-all | bytes 36864 | tf_op jit(solution)/shard_map/all_to_all | solution.py:94
  180.7 0.6 broadcast_in_dim.45
  181.3 3.3 %all-to-all-start.6 = ((bf16[8,6,384]{2,1,0:T(8,128)(2,1)}), bf16[8,6,384]{2,1,0:T(8,128)(2,1)S(1)}, u32[]{:S(2)}, u32[]{:S(2)}) async-start(bf16[8,6,384]{2,1,0:T(8,128)(2,1)} %broadcast_in_dim.45), calls=%async_computation.6 | async-start | bytes 98304 | tf_op jit(solution)/shard_map/all_to_all | solution.py:96
  184.7 0.8 copy.12
  185.4 5.8 %all-to-all-done.6 = bf16[8,6,384]{2,1,0:T(8,128)(2,1)S(1)} async-done(((bf16[8,6,384]{2,1,0:T(8,128)(2,1)}), bf16[8,6,384]{2,1,0:T(8,128)(2,1)S(1)}, u32[]{:S(2)}, u32[]{:S(2)}) %all-to-all-start.6) | async-done | bytes 36896 | tf_op jit(solution)/shard_map/all_to_all | solution.py:96
  191.3 0.6 reshape.53
  (25 shorter events, 0.2 us)
Async XLA Ops:
  0.6 0.8 copy-start
  2.0 50.0 %all-to-all-start = ((bf16[4,3,384]{2,1,0:T(4,128)(2,1)}), bf16[4,3,384]{2,1,0:T(4,128)(2,1)S(1)}, u32[]{:S(2)}, u32[]{:S(2)}) async-start(bf16[4,3,384]{2,1,0:T(4,128)(2,1)} %broadcast_in_dim.38), calls=%async_computation | async-start | bytes 24576 | tf_op jit(solution)/shard_map/all_to_all | solution.py:72
  31.0 3.0 %copy-start.5 = (bf16[512,3072]{1,0:T(8,128)(2,1)S(1)}, bf16[512,3072]{1,0:T(8,128)(2,1)}, u32[]{:S(2)}) copy-start(bf16[512,3072]{1,0:T(8,128)(2,1)} %param.5) | copy-start | bytes 9437188
  52.7 14.7 %all-to-all-start.1 = ((bf16[8,12,384]{2,1,0:T(8,128)(2,1)}), bf16[8,12,384]{2,1,0:T(8,128)(2,1)S(1)}, u32[]{:S(2)}, u32[]{:S(2)}) async-start(bf16[8,12,384]{2,1,0:T(8,128)(2,1)} %broadcast_in_dim.39), calls=%async_computation.1 | async-start | bytes 196608 | tf_op jit(solution)/shard_map/all_to_all | solution.py:74
  57.4 1.1 copy-start.2
  58.5 37.2 %copy-start.4 = (s32[1,4,4]{2,1,0:T(4,128)S(1)}, s32[1,4,4]{2,1,0:T(4,128)}, u32[]{:S(2)}) copy-start(s32[1,4,4]{2,1,0:T(4,128)} %param.8) | copy-start | bytes 196
  58.5 38.1 %copy-start.1 = (bf16[512,128]{1,0:T(8,128)(2,1)S(1)}, bf16[512,128]{1,0:T(8,128)(2,1)}, u32[]{:S(2)}) copy-start(bf16[512,128]{1,0:T(8,128)(2,1)} %param.7) | copy-start | bytes 393220
  89.0 10.8 %collective-permute-start = (bf16[1536,384]{1,0:T(8,128)(2,1)}, bf16[1536,384]{1,0:T(8,128)(2,1)}, u32[]{:S(2)}, u32[]{:S(2)}) collective-permute-start(bf16[1536,384]{1,0:T(8,128)(2,1)} %bitcast.7), channel_id=1, source_target_pairs={{0,64},{64,0},{1,65},{65,1},{2,66},{66,2},{3,67},{67,3},{4,68},{68... | collective-permute-start | bytes 3538952 | tf_op jit(solution)/shard_map/ppermute | solution.py:81
  102.2 0.9 copy-start.3
  105.6 4.7 %collective-permute-start.1 = (bf16[1536,384]{1,0:T(8,128)(2,1)S(1)}, bf16[1536,384]{1,0:T(8,128)(2,1)S(1)}, u32[]{:S(2)}, u32[]{:S(2)}) collective-permute-start(bf16[1536,384]{1,0:T(8,128)(2,1)S(1)} %convolution_convert_fusion), channel_id=1, source_target_pairs={{0,64},{64,0},{1,65},{65,1},{2,66},{66,2},{3,67},{67,3},{4,68},{68... | collective-permute-start | bytes 3538952 | tf_op jit(solution)/shard_map/ppermute | solution.py:87
  181.3 9.9 %all-to-all-start.6 = ((bf16[8,6,384]{2,1,0:T(8,128)(2,1)}), bf16[8,6,384]{2,1,0:T(8,128)(2,1)S(1)}, u32[]{:S(2)}, u32[]{:S(2)}) async-start(bf16[8,6,384]{2,1,0:T(8,128)(2,1)} %broadcast_in_dim.45), calls=%async_computation.6 | async-start | bytes 98304 | tf_op jit(solution)/shard_map/all_to_all | solution.py:96

commit v3 on v1

v3 whole, which is shorter than its diff:
```python
import math

import jax
import jax.numpy as jnp
from jax import lax
from jax.experimental import pallas as pl
from jax.experimental.pallas import tpu as pltpu
from jax.sharding import Mesh
from jax.sharding import PartitionSpec as P

BF16 = jnp.bfloat16
F32 = jnp.float32
DP = ("y", "xh", "core")
SHARD = ("xl", "z")
PLANE = ("y", "xh", "core", "xl")
SWAP = [(0, 1), (1, 0)]
NT = (((1,), (1,)), ((), ()))
TN = (((0,), (0,)), ((), ()))


def dot(a, b, dims=(((1,), (0,)), ((), ()))):
    return lax.dot_general(a, b, dims, preferred_element_type=F32)


def attention_kernel(mask, count, mine, passed, cotangent, attended, d_qkv):
    length, head = cotangent.shape
    blocks = mask.shape[0]
    block = length // blocks
    factor = F32(1.0 / math.sqrt(head))
    qkv = (mine[...] + passed[...]).astype(BF16)
    keys, values = qkv[:, head : 2 * head], qkv[:, 2 * head :]
    position = lax.broadcasted_iota(jnp.int32, (block, length), 1)
    grad_keys = jnp.zeros((length, head), F32)
    grad_values = jnp.zeros((length, head), F32)
    for b in range(blocks):
        rows = slice(b * block, (b + 1) * block)
        query, cot = qkv[rows, :head], cotangent[rows, :]
        limit = jnp.concatenate(
            [
                jnp.full((block, block), jnp.where(mask[b, j] > 0, count[0], 0), jnp.int32)
                for j in range(blocks)
            ],
            axis=1,
        )
        live = position < limit
        scores = jnp.where(live, dot(query, keys, NT) * factor, F32(-1e30))
        top = jnp.max(scores, axis=1, keepdims=True)
        weight = jnp.where(live, jnp.exp(scores - top), F32(0.0))
        probs = weight / jnp.sum(weight, axis=1, keepdims=True)
        probs_b = probs.astype(BF16)
        out = dot(probs_b, values).astype(BF16)
        attended[rows, :] = out
        delta = jnp.sum(cot.astype(F32) * out.astype(F32), axis=1, keepdims=True)
        dscore = (probs * (dot(cot, values, NT) - delta) * factor).astype(BF16)
        d_qkv[rows, :head] = dot(dscore, keys).astype(BF16)
        grad_keys += dot(dscore, query, TN)
        grad_values += dot(probs_b, cot, TN)
    d_qkv[:, head : 2 * head] = grad_keys.astype(BF16)
    d_qkv[:, 2 * head :] = grad_values.astype(BF16)


def attention_pass(mine, passed, cotangent, mask, count):
    length, head = cotangent.shape
    vmem = pl.BlockSpec(memory_space=pltpu.VMEM)
    smem = pl.BlockSpec(memory_space=pltpu.SMEM)
    return pl.pallas_call(
        attention_kernel,
        out_shape=(
            jax.ShapeDtypeStruct((length, head), BF16),
            jax.ShapeDtypeStruct((length, 3 * head), BF16),
        ),
        in_specs=[smem, smem, vmem, vmem, vmem],
        out_specs=(vmem, vmem),
        compiler_params=pltpu.CompilerParams(vmem_limit_bytes=24 * 1024 * 1024),
        cost_estimate=pl.CostEstimate(
            flops=14 * length * length * head, bytes_accessed=2 * 1024 * 1024, transcendentals=length * length
        ),
        name="attention",
    )(mask, count, mine, passed, cotangent)


def z_at(place, n_z):
    return (place // 2 + n_z // 2 * (1 - place % 2)) % n_z


def replica_at(place):
    return (place // 4 + 2) % 4, 1 - place // 2 % 2, place % 2


def index(y, xh, core, xl):
    return ((y * 2 + xh) * 2 + core) * 2 + xl


def groups():
    places = [replica_at(p) for p in range(16)]
    chips = [[index(*places[2 * p][:2], core, xl) for xl in range(2) for p in range(8)] for core in range(2)]
    replicas = [[index(*place, xl) for place in places] for xl in range(2)]
    return [[z_at(p, 32) for p in range(32)]], chips, replicas


def reordered(feats, core, n_xl, n_z, n_dp, unit):
    depth = feats.shape[1] // n_xl
    line = n_z * unit
    at = lax.broadcasted_iota(jnp.int32, (depth, depth // 2), 1)
    pair, z, row = at // line, z_at((at % line) // unit, n_z), at % unit
    source = z * (n_dp * unit) + (2 * pair + core) * unit + row
    pick = (lax.broadcasted_iota(jnp.int32, (depth, depth // 2), 0) == source).astype(BF16)
    blocks = [dot(feats[:, k * depth : (k + 1) * depth], pick).astype(BF16) for k in range(n_xl)]
    return jnp.concatenate(blocks, axis=1)


def on_device(feats, w_qkv, grad_out, block_mask, counts):
    n_xl, n_z, n_dp = lax.axis_size("xl"), lax.axis_size("z"), lax.axis_size(DP)
    chips = 16
    rows, width = w_qkv.shape
    unit = rows // n_dp
    core = lax.axis_index("core")

    theirs = lax.ppermute(reordered(feats, 1 - core, n_xl, n_z, n_dp, unit), "core", SWAP)
    own_feats = reordered(feats, core, n_xl, n_z, n_dp, unit)

    lines, plane_chips, replicas = groups()
    place = (lax.axis_index("y") + 2) % 4 * 4 + (1 - lax.axis_index("xh")) * 2 + core
    piece = lax.dynamic_slice_in_dim(w_qkv, place * unit, unit, axis=0)
    line = lax.all_to_all(jnp.broadcast_to(piece, (n_z, unit, width)), "z", 0, 0, axis_index_groups=lines, tiled=True)
    line = line.reshape(n_z * unit, width)
    line, theirs, own_feats = lax.optimization_barrier((line, theirs, own_feats))
    own_w = lax.all_to_all(jnp.broadcast_to(line, (chips,) + line.shape), PLANE, 0, 0, axis_index_groups=plane_chips, tiled=True)
    own_w = own_w.reshape(chips * n_z * unit, width)

    passed = lax.ppermute(dot(theirs, own_w), "core", SWAP)
    attended, d_qkv = attention_pass(dot(own_feats, own_w), passed, grad_out, block_mask[0], counts)

    d_theirs = lax.ppermute(d_qkv, "core", SWAP)
    own_part = lax.optimization_barrier(dot(own_feats, d_qkv, TN))
    chip = (own_part + dot(theirs, d_theirs, TN)).astype(BF16)
    plane = lax.all_to_all(chip.reshape(chips, n_z * unit, width), PLANE, 0, 0, axis_index_groups=plane_chips, tiled=True)
    plane = jnp.sum(plane.astype(F32), axis=0).astype(BF16)
    owned = lax.all_to_all(plane.reshape(n_z, unit, width), "z", 0, 0, axis_index_groups=lines, tiled=True)
    owned = jnp.sum(owned.astype(F32), axis=0).astype(BF16)
    grad_w = lax.all_to_all(jnp.broadcast_to(owned, (n_dp, unit, width)), PLANE, 0, 0, axis_index_groups=replicas, tiled=True)
    return (attended, grad_w.reshape(rows, width).astype(F32))


def solution(mesh):
    fine = Mesh(mesh.devices.reshape(4, 2, 2, 2, 32), DP + SHARD)
    split = DP + SHARD
    return jax.shard_map(
        on_device,
        mesh=fine,
        in_specs=(
            P(split, None),
            P(SHARD, None),
            P(split, None),
            P(split, None, None),
            P(split),
        ),
        out_specs=(P(split, None), P(SHARD, None)),
        check_vma=False,
    )
```

time: 170 us -> 150 us (0.88)
  waiting for transfers between devices: 40.7 us -> 0.47 us
  blocking collectives: 50.9 us -> 83.7 us
  starting transfers between devices: 52.6 us -> 44.7 us
  matrix products: 17 us -> 11.4 us
  Pallas kernels: 0 us -> 3.72 us
  local copies, waits for them, and re-layouts: 5.14 us -> 2.33 us
    all_to_all x3 -> x1, waiting for transfers between devices: 37.9 us -> 0.01 us  [on_device(): lax.all_to_all(jnp.broadcast_to(piece, (n_z, unit, width)), 'z', 0, 0, ax...]
    all_to_all x2 -> x4, blocking collectives: 50.9 us -> 83.7 us  [the longest x1 30.2 us: on_device(): lax.all_to_all(plane.reshape(n_z, unit, width), 'z', 0, 0, axis_index_gro...]
    all_to_all x3 -> x1, starting transfers between devices: 44.2 us -> 36.2 us  [on_device(): lax.all_to_all(jnp.broadcast_to(piece, (n_z, unit, width)), 'z', 0, 0, ax...]
    dot_general x14 -> x8, matrix products: 17 us -> 11.4 us  [dot(): return lax.dot_general(a, b, dims, preferred_element_type=F32)]
    pallas_call x0 -> x1, Pallas kernels: none -> 3.72 us  [attention_pass(): pl.pallas_call(attention_kernel, out_shape=(jax.ShapeDtypeStruct((length,...]
    ppermute x2 -> x3, waiting for transfers between devices: 2.81 us -> 0.47 us  [the longest x1 0.23 us: on_device(): passed = lax.ppermute(dot(theirs, own_w), 'core', SWAP)]
    ppermute x2 -> x3, starting transfers between devices: 8.46 us -> 8.56 us  [the longest x1 3.13 us: on_device(): lax.ppermute(reordered(feats, 1 - core, n_xl, n_z, n_dp, unit), 'core', S...]
  transfers between devices with their start and end apart: 5 -> 4, of which waited for: 4 -> 3; matrix products, arithmetic and copies ran while one was open for 8% -> 7% of each run, Pallas kernels for 0% -> 0%
where the time goes in v3:
time: 150 us
  blocking collectives  83.7 us (56%)
  starting transfers between devices  44.7 us (30%)
  matrix products  11.4 us (8%)
  Pallas kernels  3.72 us (2%)
  local copies, waits for them, and re-layouts  2.33 us (2%)
  other arithmetic  1.96 us (1%)
    all_to_all x1, starting transfers between devices, on_device(): lax.all_to_all(jnp.broadcast_to(piece, (n_z, unit, width)), 'z', 0, 0, ax...  36.2 us
    all_to_all x1, blocking collectives, on_device(): lax.all_to_all(plane.reshape(n_z, unit, width), 'z', 0, 0, axis_index_gro...  30.2 us
    all_to_all x1, blocking collectives, on_device(): lax.all_to_all(jnp.broadcast_to(line, (chips,) + line.shape), PLANE, 0, 0...  21.9 us
    all_to_all x1, blocking collectives, on_device(): lax.all_to_all(chip.reshape(chips, n_z * unit, width), PLANE, 0, 0, axis_...  21.3 us
    dot_general x8, matrix products, dot(): return lax.dot_general(a, b, dims, preferred_element_type=F32)  11.4 us
    all_to_all x1, blocking collectives, on_device(): lax.all_to_all(jnp.broadcast_to(owned, (n_dp, unit, width)), PLANE, 0, 0,...  10.2 us
    pallas_call x1, Pallas kernels, attention_pass(): pl.pallas_call(attention_kernel, out_shape=(jax.ShapeDtypeStruct((length,...  3.72 us
    ppermute x1, starting transfers between devices, on_device(): lax.ppermute(reordered(feats, 1 - core, n_xl, n_z, n_dp, unit), 'core', S...  3.13 us
  transfers between devices with their start and end apart: 4, of which 3 were waited for; matrix products, arithmetic and copies ran while one was open for 7% of the time, Pallas kernels for 0%

profile of v3, /device:TPU:1, one launch (start us, length us, event | category | flops | bytes accessed | tf_op | source)
XLA Modules:
  0.0 149.8 jit_solution(3295395224324802864)
XLA Ops:
  0.6 0.0 copy-start
  0.7 0.7 copy-done
  1.4 0.7 broadcast_in_dim.9
  2.1 36.2 %all-to-all-start = ((bf16[32,3,384]{2,1,0:T(4,128)(2,1)}), bf16[32,3,384]{2,1,0:T(4,128)(2,1)S(1)}, u32[]{:S(2)}, u32[]{:S(2)}) async-start(bf16[32,3,384]{2,1,0:T(4,128)(2,1)} %broadcast_in_dim.9), calls=%async_computation | async-start | bytes 196608 | tf_op jit(solution)/shard_map/all_to_all | solution.py:125
  38.3 0.0 copy-start.3
  38.3 3.0 %fusion.23 = bf16[512,768]{0,1:T(8,128)(2,1)S(1)} fusion(bf16[512,3072]{1,0:T(8,128)(2,1)} %param.5, s32[768]{0:T(1024)S(1)} %get-tuple-element.13, s32[768]{0:T(1024)S(1)} %get-tuple-element.14, s32[]{:T(128)S(6)} %sub.44, s32[768]{0:T(1024)S(1)} %get-tuple-element.12, s32[768]{0:T(1024)S(1)} %get-tuple-element.17, pred[768]{0:T(1024)(128)(4,1)S(1)} %fusion.45, ...), kind=kOutput, calls=%fused_computation.44 | convolution fusion | flops 1269694464 | bytes 2380036 | tf_op jit(solution)/shard_map/dot_general | solution.py:22
  41.4 0.0 copy-done.3
  41.4 1.5 fusion.20
  42.9 1.3 pad_maximum_fusion
  44.1 3.1 %collective-permute-start = (bf16[512,1536]{0,1:T(8,128)(2,1)}, bf16[512,1536]{0,1:T(8,128)(2,1)S(1)}, u32[]{:S(2)}, u32[]{:S(2)}) collective-permute-start(bf16[512,1536]{0,1:T(8,128)(2,1)} %pad_maximum_fusion), channel_id=1, source_target_pairs={{0,64},{64,0},{1,65},{65,1},{2,66},{66,2},{3,67},{67,3},{4,68},{68... | collective-permute-start | bytes 4718600 | tf_op jit(solution)/shard_map/ppermute | solution.py:119
  47.2 1.5 fusion.26
  48.7 1.5 fusion.29
  50.2 0.1 pad_maximum_fusion.1
  50.3 0.0 all-to-all-done
  50.3 0.1 reshape.19
  50.4 0.1 collective-permute-done
  50.5 0.1 broadcast_in_dim.10
  50.6 21.9 %all_to_all.25 = bf16[16,96,384]{2,1,0:T(8,128)(2,1)S(1)} all-to-all(bf16[16,96,384]{2,1,0:T(8,128)(2,1)S(1)} %broadcast_in_dim.10), channel_id=1, replica_groups={{640,512,896,768,128,0,384,256,672,544,928,800,160,32,416,288},{704,576..., dimensions={0} | all-to-all | bytes 2359296 | tf_op jit(solution)/shard_map/all_to_all | solution.py:128
  72.5 1.0 fusion.83
  73.5 0.0 copy-start.1
  73.5 0.0 copy-start.2
  73.5 3.0 %collective-permute-start.1 = (f32[512,384]{1,0:T(8,128)S(1)}, f32[512,384]{1,0:T(8,128)S(1)}, u32[]{:S(2)}, u32[]{:S(2)}) collective-permute-start(f32[512,384]{1,0:T(8,128)S(1)} %fusion.83), channel_id=1, source_target_pairs={{0,64},{64,0},{1,65},{65,1},{2,66},{66,2},{3,67},{67,3},{4,68},{68... | collective-permute-start | bytes 2359304 | tf_op jit(solution)/shard_map/ppermute | solution.py:131
  77.2 1.0 fusion.82.mine
  78.2 0.2 collective-permute-done.1.passed
  78.4 0.0 copy-done.1
  78.4 0.0 copy-done.2
  78.4 3.7 %attention.1 = (bf16[512,128]{1,0:T(8,128)(2,1)}, bf16[512,384]{1,0:T(8,128)(2,1)S(1)}) custom-call(s32[4,4]{1,0:T(4,128)S(1)} %bitcast.19, s32[1]{0:T(128)S(6)} %copy.7.count, f32[512,384]{1,0:T(8,128)S(1)} %fusion.82.mine, f32[512,384]{1,0:T(8,128)S(1)} %collective-permute-done.1.passed, bf16[512,128]{1,0:T(8,128)(2,1)S(1)} %copy-done.1), custom_call_target="tpu_custom_call" | custom-call | flops 469762048 | bytes 2097152 | tf_op jit(solution)/shard_map/attention/pallas_call | solution.py:66
  82.1 2.4 %collective-permute-start.2 = (bf16[512,384]{1,0:T(8,128)(2,1)S(1)}, bf16[512,384]{1,0:T(8,128)(2,1)S(1)}, u32[]{:S(2)}, u32[]{:S(2)}) collective-permute-start(bf16[512,384]{1,0:T(8,128)(2,1)S(1)} %get-tuple-element.11), channel_id=1, source_target_pairs={{0,64},{64,0},{1,65},{65,1},{2,66},{66,2},{3,67},{67,3},{4,68},{68... | collective-permute-start | bytes 1179656 | tf_op jit(solution)/shard_map/ppermute | solution.py:134
  84.6 1.0 fusion.84
  85.6 0.2 collective-permute-done.2
  85.7 1.0 fusion.85
  86.7 0.3 add_convert_fusion
  87.1 21.3 %all_to_all.26 = bf16[16,96,384]{2,1,0:T(8,128)(2,1)S(1)} all-to-all(bf16[16,96,384]{2,1,0:T(8,128)(2,1)S(1)} %bitcast.20), channel_id=1, replica_groups={{640,512,896,768,128,0,384,256,672,544,928,800,160,32,416,288},{704,576..., dimensions={0} | all-to-all | bytes 2359296 | tf_op jit(solution)/shard_map/all_to_all | solution.py:137
  108.4 0.2 reduce_sum.24
  108.6 30.2 %all_to_all.27 = bf16[32,3,384]{2,1,0:T(4,128)(2,1)S(1)} all-to-all(bf16[32,3,384]{2,1,0:T(4,128)(2,1)S(1)} %reshape.22), channel_id=1, replica_groups={{16,0,17,1,18,2,19,3,20,4,21,5,22,6,23,7,24,8,25,9,26,10,27,11,28,12,29..., dimensions={0} | all-to-all | bytes 147456 | tf_op jit(solution)/shard_map/all_to_all | solution.py:139
  138.8 0.1 reduce_sum.25
  138.9 10.2 %all_to_all.28 = bf16[16,3,384]{2,1,0:T(4,128)(2,1)S(1)} all-to-all(bf16[16,3,384]{2,1,0:T(4,128)(2,1)S(1)} %broadcast_in_dim.11), channel_id=1, replica_groups={{640,704,512,576,896,960,768,832,128,192,0,64,384,448,256,320},{672,736..., dimensions={0} | all-to-all | bytes 73728 | tf_op jit(solution)/shard_map/all_to_all | solution.py:141
  149.2 0.7 reshape.23
  (8 shorter events, 0.1 us)
Async XLA Ops:
  0.6 0.8 copy-start
  2.1 48.2 %all-to-all-start = ((bf16[32,3,384]{2,1,0:T(4,128)(2,1)}), bf16[32,3,384]{2,1,0:T(4,128)(2,1)S(1)}, u32[]{:S(2)}, u32[]{:S(2)}) async-start(bf16[32,3,384]{2,1,0:T(4,128)(2,1)} %broadcast_in_dim.9), calls=%async_computation | async-start | bytes 196608 | tf_op jit(solution)/shard_map/all_to_all | solution.py:125
  38.3 3.1 %copy-start.3 = (bf16[512,3072]{1,0:T(8,128)(2,1)S(1)}, bf16[512,3072]{1,0:T(8,128)(2,1)}, u32[]{:S(2)}) copy-start(bf16[512,3072]{1,0:T(8,128)(2,1)} %param.5) | copy-start | bytes 9437188
  44.1 6.4 %collective-permute-start = (bf16[512,1536]{0,1:T(8,128)(2,1)}, bf16[512,1536]{0,1:T(8,128)(2,1)S(1)}, u32[]{:S(2)}, u32[]{:S(2)}) collective-permute-start(bf16[512,1536]{0,1:T(8,128)(2,1)} %pad_maximum_fusion), channel_id=1, source_target_pairs={{0,64},{64,0},{1,65},{65,1},{2,66},{66,2},{3,67},{67,3},{4,68},{68... | collective-permute-start | bytes 4718600 | tf_op jit(solution)/shard_map/ppermute | solution.py:119
  73.5 4.9 %copy-start.1 = (bf16[512,128]{1,0:T(8,128)(2,1)S(1)}, bf16[512,128]{1,0:T(8,128)(2,1)}, u32[]{:S(2)}) copy-start(bf16[512,128]{1,0:T(8,128)(2,1)} %cotangent.1) | copy-start | bytes 393220
  73.5 4.9 %copy-start.2 = (s32[1,4,4]{2,1,0:T(4,128)S(1)}, s32[1,4,4]{2,1,0:T(4,128)}, u32[]{:S(2)}) copy-start(s32[1,4,4]{2,1,0:T(4,128)} %param.8) | copy-start | bytes 196
  73.5 4.9 %collective-permute-start.1 = (f32[512,384]{1,0:T(8,128)S(1)}, f32[512,384]{1,0:T(8,128)S(1)}, u32[]{:S(2)}, u32[]{:S(2)}) collective-permute-start(f32[512,384]{1,0:T(8,128)S(1)} %fusion.83), channel_id=1, source_target_pairs={{0,64},{64,0},{1,65},{65,1},{2,66},{66,2},{3,67},{67,3},{4,68},{68... | collective-permute-start | bytes 2359304 | tf_op jit(solution)/shard_map/ppermute | solution.py:131
  82.1 3.6 %collective-permute-start.2 = (bf16[512,384]{1,0:T(8,128)(2,1)S(1)}, bf16[512,384]{1,0:T(8,128)(2,1)S(1)}, u32[]{:S(2)}, u32[]{:S(2)}) collective-permute-start(bf16[512,384]{1,0:T(8,128)(2,1)S(1)} %get-tuple-element.11), channel_id=1, source_target_pairs={{0,64},{64,0},{1,65},{65,1},{2,66},{66,2},{3,67},{67,3},{4,68},{68... | collective-permute-start | bytes 1179656 | tf_op jit(solution)/shard_map/ppermute | solution.py:134

commit v4 on v3

--- a/solution.py
+++ b/solution.py
@@ -28,35 +28,34 @@
     block = length // blocks
     factor = F32(1.0 / math.sqrt(head))
     qkv = (mine[...] + passed[...]).astype(BF16)
-    keys, values = qkv[:, head : 2 * head], qkv[:, 2 * head :]
-    position = lax.broadcasted_iota(jnp.int32, (block, length), 1)
-    grad_keys = jnp.zeros((length, head), F32)
-    grad_values = jnp.zeros((length, head), F32)
-    for b in range(blocks):
-        rows = slice(b * block, (b + 1) * block)
-        query, cot = qkv[rows, :head], cotangent[rows, :]
-        limit = jnp.concatenate(
-            [
-                jnp.full((block, block), jnp.where(mask[b, j] > 0, count[0], 0), jnp.int32)
-                for j in range(blocks)
-            ],
-            axis=1,
-        )
-        live = position < limit
-        scores = jnp.where(live, dot(query, keys, NT) * factor, F32(-1e30))
-        top = jnp.max(scores, axis=1, keepdims=True)
-        weight = jnp.where(live, jnp.exp(scores - top), F32(0.0))
-        probs = weight / jnp.sum(weight, axis=1, keepdims=True)
-        probs_b = probs.astype(BF16)
-        out = dot(probs_b, values).astype(BF16)
-        attended[rows, :] = out
-        delta = jnp.sum(cot.astype(F32) * out.astype(F32), axis=1, keepdims=True)
-        dscore = (probs * (dot(cot, values, NT) - delta) * factor).astype(BF16)
-        d_qkv[rows, :head] = dot(dscore, keys).astype(BF16)
-        grad_keys += dot(dscore, query, TN)
-        grad_values += dot(probs_b, cot, TN)
-    d_qkv[:, head : 2 * head] = grad_keys.astype(BF16)
-    d_qkv[:, 2 * head :] = grad_values.astype(BF16)
+    query, keys, values = qkv[:, :head], qkv[:, head : 2 * head], qkv[:, 2 * head :]
+    limit = jnp.concatenate(
+        [
+            jnp.concatenate(
+                [
+                    jnp.full((block, block), jnp.where(mask[i, j] > 0, count[0], 0), jnp.int32)
+                    for j in range(blocks)
+                ],
+                axis=1,
+            )
+            for i in range(blocks)
+        ],
+        axis=0,
+    )
+    live = lax.broadcasted_iota(jnp.int32, (length, length), 1) < limit
+    scores = jnp.where(live, dot(query, keys, NT) * factor, F32(-1e30))
+    top = jnp.max(scores, axis=1, keepdims=True)
+    weight = jnp.where(live, jnp.exp(scores - top), F32(0.0))
+    probs = weight / jnp.sum(weight, axis=1, keepdims=True)
+    probs_b = probs.astype(BF16)
+    out = dot(probs_b, values).astype(BF16)
+    attended[...] = out
+    cot = cotangent[...]
+    delta = jnp.sum(cot.astype(F32) * out.astype(F32), axis=1, keepdims=True)
+    dscore = (probs * (dot(cot, values, NT) - delta) * factor).astype(BF16)
+    d_qkv[:, :head] = dot(dscore, keys).astype(BF16)
+    d_qkv[:, head : 2 * head] = dot(query, dscore, TN).T.astype(BF16)
+    d_qkv[:, 2 * head :] = dot(cot, probs_b, TN).T.astype(BF16)
 
 
 def attention_pass(mine, passed, cotangent, mask, count):

time: 150 us -> 149 us (level)
  Pallas kernels: 3.72 us -> 2.14 us
    pallas_call x1, Pallas kernels: 3.72 us -> 2.14 us  [attention_pass(): pl.pallas_call(attention_kernel, out_shape=(jax.ShapeDtypeStruct((length,...]
where the time goes in v4:
time: 149 us; the launch traced here: 148 us
  blocking collectives  83.7 us (56%)
  starting transfers between devices  44.5 us (30%)
  matrix products  11.4 us (8%)
  local copies, waits for them, and re-layouts  2.33 us (2%)
  Pallas kernels  2.14 us (1%)
  other arithmetic  1.96 us (1%)
    all_to_all x1, starting transfers between devices, on_device(): lax.all_to_all(jnp.broadcast_to(piece, (n_z, unit, width)), 'z', 0, 0, ax...  36.2 us
    all_to_all x1, blocking collectives, on_device(): lax.all_to_all(plane.reshape(n_z, unit, width), 'z', 0, 0, axis_index_gro...  30.2 us
    all_to_all x1, blocking collectives, on_device(): lax.all_to_all(jnp.broadcast_to(line, (chips,) + line.shape), PLANE, 0, 0...  21.9 us
    all_to_all x1, blocking collectives, on_device(): lax.all_to_all(chip.reshape(chips, n_z * unit, width), PLANE, 0, 0, axis_...  21.3 us
    dot_general x8, matrix products, dot(): return lax.dot_general(a, b, dims, preferred_element_type=F32)  11.4 us
    all_to_all x1, blocking collectives, on_device(): lax.all_to_all(jnp.broadcast_to(owned, (n_dp, unit, width)), PLANE, 0, 0,...  10.2 us
    ppermute x1, starting transfers between devices, on_device(): lax.ppermute(reordered(feats, 1 - core, n_xl, n_z, n_dp, unit), 'core', S...  3.13 us
  transfers between devices with their start and end apart: 4, of which 3 were waited for; matrix products, arithmetic and copies ran while one was open for 7% of the time, Pallas kernels for 0%

profile of v4, /device:TPU:1, one launch (start us, length us, event | category | flops | bytes accessed | tf_op | source)
XLA Modules:
  0.0 148.2 jit_solution(531535601238885853)
XLA Ops:
  0.6 0.0 copy-start
  0.7 0.7 copy-done
  1.4 0.7 broadcast_in_dim.9
  2.1 36.2 %all-to-all-start = ((bf16[32,3,384]{2,1,0:T(4,128)(2,1)}), bf16[32,3,384]{2,1,0:T(4,128)(2,1)S(1)}, u32[]{:S(2)}, u32[]{:S(2)}) async-start(bf16[32,3,384]{2,1,0:T(4,128)(2,1)} %broadcast_in_dim.9), calls=%async_computation | async-start | bytes 196608 | tf_op jit(solution)/shard_map/all_to_all | solution.py:124
  38.3 0.0 copy-start.3
  38.3 3.0 %fusion.23 = bf16[512,768]{0,1:T(8,128)(2,1)S(1)} fusion(bf16[512,3072]{1,0:T(8,128)(2,1)} %param.5, s32[768]{0:T(1024)S(1)} %get-tuple-element.13, s32[768]{0:T(1024)S(1)} %get-tuple-element.14, s32[]{:T(128)S(6)} %sub.44, s32[768]{0:T(1024)S(1)} %get-tuple-element.12, s32[768]{0:T(1024)S(1)} %get-tuple-element.17, pred[768]{0:T(1024)(128)(4,1)S(1)} %fusion.45, ...), kind=kOutput, calls=%fused_computation.44 | convolution fusion | flops 1269694464 | bytes 2380036 | tf_op jit(solution)/shard_map/dot_general | solution.py:22
  41.4 0.0 copy-done.3
  41.4 1.5 fusion.20
  42.9 1.3 pad_maximum_fusion
  44.1 3.1 %collective-permute-start = (bf16[512,1536]{0,1:T(8,128)(2,1)}, bf16[512,1536]{0,1:T(8,128)(2,1)S(1)}, u32[]{:S(2)}, u32[]{:S(2)}) collective-permute-start(bf16[512,1536]{0,1:T(8,128)(2,1)} %pad_maximum_fusion), channel_id=1, source_target_pairs={{0,64},{64,0},{1,65},{65,1},{2,66},{66,2},{3,67},{67,3},{4,68},{68... | collective-permute-start | bytes 4718600 | tf_op jit(solution)/shard_map/ppermute | solution.py:118
  47.2 1.5 fusion.26
  48.7 1.5 fusion.29
  50.2 0.1 pad_maximum_fusion.1
  50.3 0.0 all-to-all-done
  50.3 0.1 reshape.19
  50.4 0.1 collective-permute-done
  50.5 0.1 broadcast_in_dim.10
  50.6 21.9 %all_to_all.25 = bf16[16,96,384]{2,1,0:T(8,128)(2,1)S(1)} all-to-all(bf16[16,96,384]{2,1,0:T(8,128)(2,1)S(1)} %broadcast_in_dim.10), channel_id=1, replica_groups={{640,512,896,768,128,0,384,256,672,544,928,800,160,32,416,288},{704,576..., dimensions={0} | all-to-all | bytes 2359296 | tf_op jit(solution)/shard_map/all_to_all | solution.py:127
  72.5 1.0 fusion.83
  73.5 0.0 copy-start.1
  73.5 0.0 copy-start.2
  73.5 3.0 %collective-permute-start.1 = (f32[512,384]{1,0:T(8,128)S(1)}, f32[512,384]{1,0:T(8,128)S(1)}, u32[]{:S(2)}, u32[]{:S(2)}) collective-permute-start(f32[512,384]{1,0:T(8,128)S(1)} %fusion.83), channel_id=1, source_target_pairs={{0,64},{64,0},{1,65},{65,1},{2,66},{66,2},{3,67},{67,3},{4,68},{68... | collective-permute-start | bytes 2359304 | tf_op jit(solution)/shard_map/ppermute | solution.py:130
  77.2 1.0 fusion.82.mine
  78.2 0.2 collective-permute-done.1.passed
  78.4 0.0 copy-done.1
  78.4 0.0 copy-done.2
  78.4 2.1 %attention.1 = (bf16[512,128]{1,0:T(8,128)(2,1)}, bf16[512,384]{1,0:T(8,128)(2,1)S(1)}) custom-call(s32[4,4]{1,0:T(4,128)S(1)} %bitcast.19, s32[1]{0:T(128)S(6)} %copy.7.count, f32[512,384]{1,0:T(8,128)S(1)} %fusion.82.mine, f32[512,384]{1,0:T(8,128)S(1)} %collective-permute-done.1.passed, bf16[512,128]{1,0:T(8,128)(2,1)S(1)} %copy-done.1), custom_call_target="tpu_custom_call" | custom-call | flops 469762048 | bytes 2097152 | tf_op jit(solution)/shard_map/attention/pallas_call | solution.py:65
  80.6 2.3 %collective-permute-start.2 = (bf16[512,384]{1,0:T(8,128)(2,1)S(1)}, bf16[512,384]{1,0:T(8,128)(2,1)S(1)}, u32[]{:S(2)}, u32[]{:S(2)}) collective-permute-start(bf16[512,384]{1,0:T(8,128)(2,1)S(1)} %get-tuple-element.11), channel_id=1, source_target_pairs={{0,64},{64,0},{1,65},{65,1},{2,66},{66,2},{3,67},{67,3},{4,68},{68... | collective-permute-start | bytes 1179656 | tf_op jit(solution)/shard_map/ppermute | solution.py:133
  82.8 1.0 fusion.84
  83.8 0.3 collective-permute-done.2
  84.2 1.0 fusion.85
  85.2 0.3 add_convert_fusion
  85.5 21.3 %all_to_all.26 = bf16[16,96,384]{2,1,0:T(8,128)(2,1)S(1)} all-to-all(bf16[16,96,384]{2,1,0:T(8,128)(2,1)S(1)} %bitcast.20), channel_id=1, replica_groups={{640,512,896,768,128,0,384,256,672,544,928,800,160,32,416,288},{704,576..., dimensions={0} | all-to-all | bytes 2359296 | tf_op jit(solution)/shard_map/all_to_all | solution.py:136
  106.8 0.2 reduce_sum.24
  107.0 30.2 %all_to_all.27 = bf16[32,3,384]{2,1,0:T(4,128)(2,1)S(1)} all-to-all(bf16[32,3,384]{2,1,0:T(4,128)(2,1)S(1)} %reshape.22), channel_id=1, replica_groups={{16,0,17,1,18,2,19,3,20,4,21,5,22,6,23,7,24,8,25,9,26,10,27,11,28,12,29..., dimensions={0} | all-to-all | bytes 147456 | tf_op jit(solution)/shard_map/all_to_all | solution.py:138
  137.3 0.1 reduce_sum.25
  137.3 10.2 %all_to_all.28 = bf16[16,3,384]{2,1,0:T(4,128)(2,1)S(1)} all-to-all(bf16[16,3,384]{2,1,0:T(4,128)(2,1)S(1)} %broadcast_in_dim.11), channel_id=1, replica_groups={{640,704,512,576,896,960,768,832,128,192,0,64,384,448,256,320},{672,736..., dimensions={0} | all-to-all | bytes 73728 | tf_op jit(solution)/shard_map/all_to_all | solution.py:140
  147.6 0.7 reshape.23
  (8 shorter events, 0.1 us)
Async XLA Ops:
  0.6 0.8 copy-start
  2.1 48.2 %all-to-all-start = ((bf16[32,3,384]{2,1,0:T(4,128)(2,1)}), bf16[32,3,384]{2,1,0:T(4,128)(2,1)S(1)}, u32[]{:S(2)}, u32[]{:S(2)}) async-start(bf16[32,3,384]{2,1,0:T(4,128)(2,1)} %broadcast_in_dim.9), calls=%async_computation | async-start | bytes 196608 | tf_op jit(solution)/shard_map/all_to_all | solution.py:124
  38.3 3.1 %copy-start.3 = (bf16[512,3072]{1,0:T(8,128)(2,1)S(1)}, bf16[512,3072]{1,0:T(8,128)(2,1)}, u32[]{:S(2)}) copy-start(bf16[512,3072]{1,0:T(8,128)(2,1)} %param.5) | copy-start | bytes 9437188
  44.1 6.4 %collective-permute-start = (bf16[512,1536]{0,1:T(8,128)(2,1)}, bf16[512,1536]{0,1:T(8,128)(2,1)S(1)}, u32[]{:S(2)}, u32[]{:S(2)}) collective-permute-start(bf16[512,1536]{0,1:T(8,128)(2,1)} %pad_maximum_fusion), channel_id=1, source_target_pairs={{0,64},{64,0},{1,65},{65,1},{2,66},{66,2},{3,67},{67,3},{4,68},{68... | collective-permute-start | bytes 4718600 | tf_op jit(solution)/shard_map/ppermute | solution.py:118
  73.5 4.9 %copy-start.1 = (bf16[512,128]{1,0:T(8,128)(2,1)S(1)}, bf16[512,128]{1,0:T(8,128)(2,1)}, u32[]{:S(2)}) copy-start(bf16[512,128]{1,0:T(8,128)(2,1)} %cotangent.1) | copy-start | bytes 393220
  73.5 4.9 %copy-start.2 = (s32[1,4,4]{2,1,0:T(4,128)S(1)}, s32[1,4,4]{2,1,0:T(4,128)}, u32[]{:S(2)}) copy-start(s32[1,4,4]{2,1,0:T(4,128)} %param.8) | copy-start | bytes 196
  73.5 4.9 %collective-permute-start.1 = (f32[512,384]{1,0:T(8,128)S(1)}, f32[512,384]{1,0:T(8,128)S(1)}, u32[]{:S(2)}, u32[]{:S(2)}) collective-permute-start(f32[512,384]{1,0:T(8,128)S(1)} %fusion.83), channel_id=1, source_target_pairs={{0,64},{64,0},{1,65},{65,1},{2,66},{66,2},{3,67},{67,3},{4,68},{68... | collective-permute-start | bytes 2359304 | tf_op jit(solution)/shard_map/ppermute | solution.py:130
  80.6 3.6 %collective-permute-start.2 = (bf16[512,384]{1,0:T(8,128)(2,1)S(1)}, bf16[512,384]{1,0:T(8,128)(2,1)S(1)}, u32[]{:S(2)}, u32[]{:S(2)}) collective-permute-start(bf16[512,384]{1,0:T(8,128)(2,1)S(1)} %get-tuple-element.11), channel_id=1, source_target_pairs={{0,64},{64,0},{1,65},{65,1},{2,66},{66,2},{3,67},{67,3},{4,68},{68... | collective-permute-start | bytes 1179656 | tf_op jit(solution)/shard_map/ppermute | solution.py:133

commit v5 on v4

--- a/solution.py
+++ b/solution.py
@@ -13,6 +13,7 @@
 DP = ("y", "xh", "core")
 SHARD = ("xl", "z")
 PLANE = ("y", "xh", "core", "xl")
+AHEAD = 4
 SWAP = [(0, 1), (1, 0)]
 NT = (((1,), (1,)), ((), ()))
 TN = (((0,), (0,)), ((), ()))
@@ -79,7 +80,7 @@
 
 
 def z_at(place, n_z):
-    return (place // 2 + n_z // 2 * (1 - place % 2)) % n_z
+    return (place + n_z // 2) % n_z
 
 
 def replica_at(place):
@@ -94,7 +95,7 @@
     places = [replica_at(p) for p in range(16)]
     chips = [[index(*places[2 * p][:2], core, xl) for xl in range(2) for p in range(8)] for core in range(2)]
     replicas = [[index(*place, xl) for place in places] for xl in range(2)]
-    return [[z_at(p, 32) for p in range(32)]], chips, replicas
+    return [[z_at(p + AHEAD, 32) for p in range(32)]], [[z_at(p, 32) for p in range(32)]], chips, replicas
 
 
 def reordered(feats, core, n_xl, n_z, n_dp, unit):
@@ -118,11 +119,11 @@
     theirs = lax.ppermute(reordered(feats, 1 - core, n_xl, n_z, n_dp, unit), "core", SWAP)
     own_feats = reordered(feats, core, n_xl, n_z, n_dp, unit)
 
-    lines, plane_chips, replicas = groups()
+    lines_in, lines_back, plane_chips, replicas = groups()
     place = (lax.axis_index("y") + 2) % 4 * 4 + (1 - lax.axis_index("xh")) * 2 + core
     piece = lax.dynamic_slice_in_dim(w_qkv, place * unit, unit, axis=0)
-    line = lax.all_to_all(jnp.broadcast_to(piece, (n_z, unit, width)), "z", 0, 0, axis_index_groups=lines, tiled=True)
-    line = line.reshape(n_z * unit, width)
+    line = lax.all_to_all(jnp.broadcast_to(piece, (n_z, unit, width)), "z", 0, 0, axis_index_groups=lines_in, tiled=True)
+    line = jnp.roll(line, AHEAD, axis=0).reshape(n_z * unit, width)
     line, theirs, own_feats = lax.optimization_barrier((line, theirs, own_feats))
     own_w = lax.all_to_all(jnp.broadcast_to(line, (chips,) + line.shape), PLANE, 0, 0, axis_index_groups=plane_chips, tiled=True)
     own_w = own_w.reshape(chips * n_z * unit, width)
@@ -135,7 +136,7 @@
     chip = (own_part + dot(theirs, d_theirs, TN)).astype(BF16)
     plane = lax.all_to_all(chip.reshape(chips, n_z * unit, width), PLANE, 0, 0, axis_index_groups=plane_chips, tiled=True)
     plane = jnp.sum(plane.astype(F32), axis=0).astype(BF16)
-    owned = lax.all_to_all(plane.reshape(n_z, unit, width), "z", 0, 0, axis_index_groups=lines, tiled=True)
+    owned = lax.all_to_all(plane.reshape(n_z, unit, width), "z", 0, 0, axis_index_groups=lines_back, tiled=True)
     owned = jnp.sum(owned.astype(F32), axis=0).astype(BF16)
     grad_w = lax.all_to_all(jnp.broadcast_to(owned, (n_dp, unit, width)), PLANE, 0, 0, axis_index_groups=replicas, tiled=True)
     return (attended, grad_w.reshape(rows, width).astype(F32))

time: 149 us -> 146 us (0.980)
  starting transfers between devices: 44.5 us -> 39.7 us
    all_to_all x1, starting transfers between devices: 36.2 us -> 31.4 us  [on_device(): lax.all_to_all(jnp.broadcast_to(piece, (n_z, unit, width)), 'z', 0, 0, ax...]
  transfers between devices with their start and end apart: 4 -> 4, of which waited for: 3 -> 3; matrix products, arithmetic and copies ran while one was open for 7% -> 8% of each run, Pallas kernels for 0% -> 0%
where the time goes in v5:
time: 146 us
  blocking collectives  84.6 us (58%)
  starting transfers between devices  39.7 us (27%)
  matrix products  11.4 us (8%)
  local copies, waits for them, and re-layouts  2.37 us (2%)
  Pallas kernels  2.11 us (1%)
  other arithmetic  2.02 us (1%)
  waiting for transfers between devices  1.86 us (1%)
  between operations  1.5 us (1%)
    all_to_all x1, starting transfers between devices, on_device(): lax.all_to_all(jnp.broadcast_to(piece, (n_z, unit, width)), 'z', 0, 0, ax...  31.4 us
    all_to_all x1, blocking collectives, on_device(): lax.all_to_all(plane.reshape(n_z, unit, width), 'z', 0, 0, axis_index_gro...  30.7 us
    all_to_all x1, blocking collectives, on_device(): lax.all_to_all(jnp.broadcast_to(line, (chips,) + line.shape), PLANE, 0, 0...  21.9 us
    all_to_all x1, blocking collectives, on_device(): lax.all_to_all(chip.reshape(chips, n_z * unit, width), PLANE, 0, 0, axis_...  21.3 us
    dot_general x8, matrix products, dot(): return lax.dot_general(a, b, dims, preferred_element_type=F32)  11.4 us
    all_to_all x1, blocking collectives, on_device(): lax.all_to_all(jnp.broadcast_to(owned, (n_dp, unit, width)), PLANE, 0, 0,...  10.7 us
    ppermute x1, starting transfers between devices, on_device(): lax.ppermute(reordered(feats, 1 - core, n_xl, n_z, n_dp, unit), 'core', S...  3.13 us
    ppermute x1, starting transfers between devices, on_device(): passed = lax.ppermute(dot(theirs, own_w), 'core', SWAP)  2.97 us
  transfers between devices with their start and end apart: 4, of which 3 were waited for; matrix products, arithmetic and copies ran while one was open for 8% of the time, Pallas kernels for 0%

profile of v5, /device:TPU:1, one launch (start us, length us, event | category | flops | bytes accessed | tf_op | source)
XLA Modules:
  0.0 145.6 jit_solution(1557524487344367356)
XLA Ops:
  0.6 0.0 copy-start
  0.7 0.7 copy-done
  1.4 0.7 broadcast_in_dim.9
  2.1 31.4 %all-to-all-start = ((bf16[32,3,384]{2,1,0:T(4,128)(2,1)}), bf16[32,3,384]{2,1,0:T(4,128)(2,1)S(1)}, u32[]{:S(2)}, u32[]{:S(2)}) async-start(bf16[32,3,384]{2,1,0:T(4,128)(2,1)} %broadcast_in_dim.9), calls=%async_computation | async-start | bytes 196608 | tf_op jit(solution)/shard_map/all_to_all | solution.py:125
  33.5 0.0 copy-start.3
  33.5 3.0 %fusion.17 = bf16[512,768]{0,1:T(8,128)(2,1)S(1)} fusion(bf16[512,3072]{1,0:T(8,128)(2,1)} %param.5, s32[768]{0:T(1024)S(1)} %get-tuple-element.13, s32[768]{0:T(1024)S(1)} %get-tuple-element.14, s32[]{:T(128)S(6)} %sub.28, s32[768]{0:T(1024)S(1)} %get-tuple-element.12, s32[768]{0:T(1024)S(1)} %get-tuple-element.17, pred[768]{0:T(1024)(128)(4,1)S(1)} %fusion.39, ...), kind=kOutput, calls=%fused_computation.32 | convolution fusion | flops 1244921856 | bytes 2380036 | tf_op jit(solution)/shard_map/dot_general | solution.py:23
  36.6 0.0 copy-done.3
  36.6 1.5 %fusion.14 = bf16[512,768]{0,1:T(8,128)(2,1)S(1)} fusion(bf16[512,3072]{1,0:T(8,128)(2,1)S(1)} %copy-done.3, s32[768]{0:T(1024)S(1)} %get-tuple-element.13, s32[768]{0:T(1024)S(1)} %get-tuple-element.14, s32[]{:T(128)S(6)} %sub.28, s32[768]{0:T(1024)S(1)} %get-tuple-element.12, s32[768]{0:T(1024)S(1)} %get-tuple-element.17, pred[768]{0:T(1024)(128)(4,1)S(1)} %fusion.39, ...), kind=kOutput, calls=%fused_computation.31 | convolution fusion | flops 1244921856 | bytes 2386948 | tf_op jit(solution)/shard_map/dot_general | solution.py:23
  38.0 1.3 pad_maximum_fusion
  39.3 3.1 %collective-permute-start = (bf16[512,1536]{0,1:T(8,128)(2,1)}, bf16[512,1536]{0,1:T(8,128)(2,1)S(1)}, u32[]{:S(2)}, u32[]{:S(2)}) collective-permute-start(bf16[512,1536]{0,1:T(8,128)(2,1)} %pad_maximum_fusion), channel_id=1, source_target_pairs={{0,64},{64,0},{1,65},{65,1},{2,66},{66,2},{3,67},{67,3},{4,68},{68... | collective-permute-start | bytes 4718600 | tf_op jit(solution)/shard_map/ppermute | solution.py:119
  42.4 1.5 %fusion.20 = bf16[512,768]{0,1:T(8,128)(2,1)S(1)} fusion(bf16[512,3072]{1,0:T(8,128)(2,1)S(1)} %copy-done.3, s32[]{:T(128)S(6)} %axis_index.41, s32[768]{0:T(1024)S(1)} %get-tuple-element.13, s32[768]{0:T(1024)S(1)} %get-tuple-element.14, s32[768]{0:T(1024)S(1)} %get-tuple-element.12, s32[768]{0:T(1024)S(1)} %get-tuple-element.17, ...), kind=kOutput, calls=%fused_computation.33 | convolution fusion | flops 1244921856 | bytes 2386948 | tf_op jit(solution)/shard_map/dot_general | solution.py:23
  43.9 1.5 %fusion.23 = bf16[512,768]{0,1:T(8,128)(2,1)S(1)} fusion(bf16[512,3072]{1,0:T(8,128)(2,1)S(1)} %copy-done.3, s32[]{:T(128)S(6)} %axis_index.41, s32[768]{0:T(1024)S(1)} %get-tuple-element.13, s32[768]{0:T(1024)S(1)} %get-tuple-element.14, s32[768]{0:T(1024)S(1)} %get-tuple-element.12, s32[768]{0:T(1024)S(1)} %get-tuple-element.17, ...), kind=kOutput, calls=%fused_computation.34 | convolution fusion | flops 1244921856 | bytes 2386948 | tf_op jit(solution)/shard_map/dot_general | solution.py:23
  45.4 0.1 pad_maximum_fusion.1
  45.5 1.3 all-to-all-done
  46.8 0.1 pad_maximum_fusion.2
  46.9 0.1 reshape.19
  47.0 0.0 collective-permute-done
  47.0 0.1 broadcast_in_dim.10
  47.1 21.9 %all_to_all.25 = bf16[16,96,384]{2,1,0:T(8,128)(2,1)S(1)} all-to-all(bf16[16,96,384]{2,1,0:T(8,128)(2,1)S(1)} %broadcast_in_dim.10), channel_id=1, replica_groups={{640,512,896,768,128,0,384,256,672,544,928,800,160,32,416,288},{704,576..., dimensions={0} | all-to-all | bytes 2359296 | tf_op jit(solution)/shard_map/all_to_all | solution.py:128
  69.0 1.0 fusion.77
  70.0 0.0 copy-start.1
  70.0 0.0 copy-start.2
  70.0 3.0 %collective-permute-start.1 = (f32[512,384]{1,0:T(8,128)S(1)}, f32[512,384]{1,0:T(8,128)S(1)}, u32[]{:S(2)}, u32[]{:S(2)}) collective-permute-start(f32[512,384]{1,0:T(8,128)S(1)} %fusion.77), channel_id=1, source_target_pairs={{0,64},{64,0},{1,65},{65,1},{2,66},{66,2},{3,67},{67,3},{4,68},{68... | collective-permute-start | bytes 2359304 | tf_op jit(solution)/shard_map/ppermute | solution.py:131
  73.7 1.0 fusion.76.mine
  74.7 0.2 collective-permute-done.1.passed
  74.9 0.0 copy-done.1
  74.9 0.0 copy-done.2
  74.9 2.1 %attention.1 = (bf16[512,128]{1,0:T(8,128)(2,1)}, bf16[512,384]{1,0:T(8,128)(2,1)S(1)}) custom-call(s32[4,4]{1,0:T(4,128)S(1)} %bitcast.19, s32[1]{0:T(128)S(6)} %copy.7.count, f32[512,384]{1,0:T(8,128)S(1)} %fusion.76.mine, f32[512,384]{1,0:T(8,128)S(1)} %collective-permute-done.1.passed, bf16[512,128]{1,0:T(8,128)(2,1)S(1)} %copy-done.1), custom_call_target="tpu_custom_call" | custom-call | flops 469762048 | bytes 2097152 | tf_op jit(solution)/shard_map/attention/pallas_call | solution.py:66
  77.0 2.3 %collective-permute-start.2 = (bf16[512,384]{1,0:T(8,128)(2,1)S(1)}, bf16[512,384]{1,0:T(8,128)(2,1)S(1)}, u32[]{:S(2)}, u32[]{:S(2)}) collective-permute-start(bf16[512,384]{1,0:T(8,128)(2,1)S(1)} %get-tuple-element.11), channel_id=1, source_target_pairs={{0,64},{64,0},{1,65},{65,1},{2,66},{66,2},{3,67},{67,3},{4,68},{68... | collective-permute-start | bytes 1179656 | tf_op jit(solution)/shard_map/ppermute | solution.py:134
  79.3 1.0 fusion.78
  80.3 0.3 collective-permute-done.2
  80.6 1.0 fusion.79
  81.6 0.3 add_convert_fusion
  81.9 21.3 %all_to_all.26 = bf16[16,96,384]{2,1,0:T(8,128)(2,1)S(1)} all-to-all(bf16[16,96,384]{2,1,0:T(8,128)(2,1)S(1)} %bitcast.20), channel_id=1, replica_groups={{640,512,896,768,128,0,384,256,672,544,928,800,160,32,416,288},{704,576..., dimensions={0} | all-to-all | bytes 2359296 | tf_op jit(solution)/shard_map/all_to_all | solution.py:137
  103.3 0.2 reduce_sum.24
  103.5 30.7 %all_to_all.27 = bf16[32,3,384]{2,1,0:T(4,128)(2,1)S(1)} all-to-all(bf16[32,3,384]{2,1,0:T(4,128)(2,1)S(1)} %reshape.22), channel_id=1, replica_groups={{16,17,18,19,20,21,22,23,24,25,26,27,28,29,30,31,0,1,2,3,4,5,6,7,8,9,10..., dimensions={0} | all-to-all | bytes 147456 | tf_op jit(solution)/shard_map/all_to_all | solution.py:139
  134.1 0.1 reduce_sum.25
  134.2 10.7 %all_to_all.28 = bf16[16,3,384]{2,1,0:T(4,128)(2,1)S(1)} all-to-all(bf16[16,3,384]{2,1,0:T(4,128)(2,1)S(1)} %broadcast_in_dim.11), channel_id=1, replica_groups={{640,704,512,576,896,960,768,832,128,192,0,64,384,448,256,320},{672,736..., dimensions={0} | all-to-all | bytes 73728 | tf_op jit(solution)/shard_map/all_to_all | solution.py:141
  144.9 0.7 reshape.23
  (10 shorter events, 0.2 us)
Async XLA Ops:
  0.6 0.8 copy-start
  2.1 44.7 %all-to-all-start = ((bf16[32,3,384]{2,1,0:T(4,128)(2,1)}), bf16[32,3,384]{2,1,0:T(4,128)(2,1)S(1)}, u32[]{:S(2)}, u32[]{:S(2)}) async-start(bf16[32,3,384]{2,1,0:T(4,128)(2,1)} %broadcast_in_dim.9), calls=%async_computation | async-start | bytes 196608 | tf_op jit(solution)/shard_map/all_to_all | solution.py:125
  33.5 3.0 %copy-start.3 = (bf16[512,3072]{1,0:T(8,128)(2,1)S(1)}, bf16[512,3072]{1,0:T(8,128)(2,1)}, u32[]{:S(2)}) copy-start(bf16[512,3072]{1,0:T(8,128)(2,1)} %param.5) | copy-start | bytes 9437188
  39.3 7.7 %collective-permute-start = (bf16[512,1536]{0,1:T(8,128)(2,1)}, bf16[512,1536]{0,1:T(8,128)(2,1)S(1)}, u32[]{:S(2)}, u32[]{:S(2)}) collective-permute-start(bf16[512,1536]{0,1:T(8,128)(2,1)} %pad_maximum_fusion), channel_id=1, source_target_pairs={{0,64},{64,0},{1,65},{65,1},{2,66},{66,2},{3,67},{67,3},{4,68},{68... | collective-permute-start | bytes 4718600 | tf_op jit(solution)/shard_map/ppermute | solution.py:119
  70.0 4.9 %copy-start.1 = (bf16[512,128]{1,0:T(8,128)(2,1)S(1)}, bf16[512,128]{1,0:T(8,128)(2,1)}, u32[]{:S(2)}) copy-start(bf16[512,128]{1,0:T(8,128)(2,1)} %cotangent.1) | copy-start | bytes 393220
  70.0 4.9 %copy-start.2 = (s32[1,4,4]{2,1,0:T(4,128)S(1)}, s32[1,4,4]{2,1,0:T(4,128)}, u32[]{:S(2)}) copy-start(s32[1,4,4]{2,1,0:T(4,128)} %param.8) | copy-start | bytes 196
  70.0 4.9 %collective-permute-start.1 = (f32[512,384]{1,0:T(8,128)S(1)}, f32[512,384]{1,0:T(8,128)S(1)}, u32[]{:S(2)}, u32[]{:S(2)}) collective-permute-start(f32[512,384]{1,0:T(8,128)S(1)} %fusion.77), channel_id=1, source_target_pairs={{0,64},{64,0},{1,65},{65,1},{2,66},{66,2},{3,67},{67,3},{4,68},{68... | collective-permute-start | bytes 2359304 | tf_op jit(solution)/shard_map/ppermute | solution.py:131
  77.0 3.6 %collective-permute-start.2 = (bf16[512,384]{1,0:T(8,128)(2,1)S(1)}, bf16[512,384]{1,0:T(8,128)(2,1)S(1)}, u32[]{:S(2)}, u32[]{:S(2)}) collective-permute-start(bf16[512,384]{1,0:T(8,128)(2,1)S(1)} %get-tuple-element.11), channel_id=1, source_target_pairs={{0,64},{64,0},{1,65},{65,1},{2,66},{66,2},{3,67},{67,3},{4,68},{68... | collective-permute-start | bytes 1179656 | tf_op jit(solution)/shard_map/ppermute | solution.py:134
